TPU v7x, 32 devices: a whole 2x2x4 slice. The times are simulated.
32 devices in a mesh: member: 2 (over y), band: 4 (over x, core), lev: 4 (over z).
Axes of the slice: x: 2, y: 2, z: 4, core: 2. Of those that a mesh axis runs over, the one named last changes fastest.
Arguments:
- spec_in: bfloat16 [4, 2, 4, 640, 1281], P('member', None, 'lev', 'band'), parts along dimension 0, may hold values from -0.0048828125 to 0.0048828125
- observation_weight: bfloat16 [32, 8, 5136], P(('band', 'lev'), 'member'), parts along dimension 1, may hold values from 0.099609375 to 1
- latitude_row_length: int32 [16], replicated, may hold values from 4116 to 5136, as said below
- wave_map: int32 [640], replicated, may hold values from 0 to 639, each once
- row_map: int32 [16], replicated, may hold values from 0 to 15, as said below
Outputs:
- grid_incr: float32 [32, 2, 8, 5136], P(('band', 'lev'), None, 'member'), parts along dimension 2
- spec_grad: bfloat16 [4, 2, 4, 640, 1281], P('member', None, 'lev', 'band'), parts along dimension 0
There are 2 independent parts, one for each index of `member`. A program takes and returns all parts, laid end to end along the dimension named above; an argument that names none is the same for every part. Nothing has to cross between parts.
Inputs may be any that keep to these rules, and one draw needn't show every extreme that they name: `latitude_row_length`: row j has 4 i + 16 points for an octahedral row number i with 1025 <= i <= 1280; row 0 always has i = 1280. `wave_map`: each pair number appears once. row_map[j] is a device number band index * 4 + lev index. A quarter of the devices hold 2 rows, half hold 1 row, and a quarter hold none.
All inputs are finite; a program needn't handle non-finite values.
Results may differ from a plain program's by a relative error of at most 0.009.
Values may be sent and summed in bfloat16 or wider, within the bound.
A program may use at most 128 MiB of HBM per device.

v0:
```python
import math

import jax
import jax.numpy as jnp
from jax import lax
from jax.sharding import PartitionSpec as P

SUBW = 128


def latitudes(latitude_row_length, halves):
    cycle_no = ((latitude_row_length - 16) // 4).astype(jnp.float32)
    colat = math.pi * (cycle_no - 0.25) / (2.0 * halves + 0.5)
    north = (
        jnp.arange(latitude_row_length.shape[0], dtype=jnp.int32)
        < latitude_row_length.shape[0] // 2
    )
    return (jnp.where(north, jnp.cos(colat), -jnp.cos(colat)), jnp.log(jnp.sin(colat)))


def side_mask(pair_ids, truncation):
    column = jnp.arange(truncation + 2, dtype=jnp.int32)[None, :]
    first_side = column < truncation + 1 - pair_ids[:, None]
    return jnp.stack([first_side, jnp.logical_not(first_side)], axis=2)


def legendre(pair_ids, cos_lat, log_sin, truncation):
    columns = truncation + 2
    column = jnp.arange(columns, dtype=jnp.int32)[None, :]
    first_order = pair_ids[:, None]
    boundary = truncation + 1 - first_order
    first_side = column < boundary
    order_m = jnp.where(first_side, first_order, truncation - first_order).astype(jnp.float32)
    degree = jnp.where(first_side, first_order + column, column - 1).astype(jnp.float32)
    restart_first = column == 0
    restart_second = column == boundary
    restart = restart_first | restart_second
    counter = jnp.arange(1, truncation + 1, dtype=jnp.int32)
    log_terms = jnp.log(1.0 - 0.5 / counter.astype(jnp.float32))

    def log_start(orders):
        partial_sum = jnp.sum(
            jnp.where(counter[None, :] <= orders, log_terms[None, :], 0.0), axis=1, keepdims=True
        )
        return 0.5 * (jnp.log(orders.astype(jnp.float32) + 0.5) + partial_sum)

    first_m = first_order.astype(jnp.float32)
    second_m = (truncation - first_order).astype(jnp.float32)
    diag_first = jnp.exp(log_start(first_order) + first_m * log_sin[None, :])
    diag_second = jnp.exp(log_start(truncation - first_order) + second_m * log_sin[None, :])

    def epsilon(values):
        upper = jnp.maximum(values * values - order_m * order_m, 0.0)
        lower = jnp.maximum(4.0 * values * values - 1.0, 1.0)
        return jnp.sqrt(upper / lower)

    divisor = jnp.where(restart, 1.0, epsilon(degree))
    slope = jnp.where(restart, 0.0, 1.0 / divisor)
    lagged = jnp.where(restart, 0.0, -epsilon(degree - 1.0) / divisor)

    def advance(carry, packed):
        older, oldest = carry
        slope_c, lagged_c, first_c, second_c = packed
        recurred = slope_c[:, None] * cos_lat[None, :] * older + lagged_c[:, None] * oldest
        value = jnp.where(
            first_c[:, None], diag_first, jnp.where(second_c[:, None], diag_second, recurred)
        )
        fresh = first_c[:, None] | second_c[:, None]
        oldest = jnp.where(fresh, 0.0, older)
        return ((value, oldest), value)

    empty = jnp.zeros((pair_ids.shape[0], cos_lat.shape[0]), jnp.float32)
    packed = (slope.T, lagged.T, jnp.broadcast_to(restart_first, slope.shape).T, restart_second.T)
    _, values = lax.scan(advance, (empty, empty), packed, unroll=16)
    return jnp.transpose(values, (1, 0, 2))


def slot_table(row_map, owners, row_cap):
    onehot = (row_map[:, None] == jnp.arange(owners, dtype=jnp.int32)[None, :]).astype(jnp.int32)
    ranking = jnp.sum((jnp.cumsum(onehot, axis=0) - onehot) * onehot, axis=1)
    slot_of_row = row_map * row_cap + ranking
    chosen = slot_of_row[None, :] == jnp.arange(owners * row_cap, dtype=jnp.int32)[:, None]
    return (slot_of_row, chosen)


def wave_order(wave_map, truncation):
    doubled = jnp.repeat(wave_map, 2)
    slots = jnp.arange(doubled.shape[0], dtype=jnp.int32)
    m_of_w = jnp.where(slots % 2 == 0, doubled, truncation - doubled)
    w_of_m = jnp.zeros_like(m_of_w).at[m_of_w].set(slots)
    return (m_of_w, w_of_m)


def fourier_tables(lengths, row_points, blocks):
    safe_len = jnp.maximum(lengths, 1)[:, None, None]
    step_angle = 2.0 * math.pi / safe_len.astype(jnp.float32)
    points = jnp.arange(row_points, dtype=jnp.int32)
    inside = points[None, :, None] < lengths[:, None, None]
    inner_m = jnp.arange(SUBW, dtype=jnp.int32)
    angles = (points[None, :, None] * inner_m[None, None, :] % safe_len).astype(
        jnp.float32
    ) * step_angle
    cosine = jnp.where(inside, jnp.cos(angles), 0.0)
    sine_vals = jnp.where(inside, jnp.sin(angles), 0.0)
    trig_table = jnp.concatenate(
        [
            jnp.concatenate([cosine, -sine_vals], axis=2),
            jnp.concatenate([sine_vals, cosine], axis=2),
        ],
        axis=1,
    )
    outer_m = jnp.arange(blocks, dtype=jnp.int32) * SUBW
    twists = (points[None, None, :] * outer_m[None, :, None] % safe_len).astype(
        jnp.float32
    ) * step_angle
    return (trig_table.astype(jnp.bfloat16), jnp.cos(twists), jnp.sin(twists))


def synthesize(coefficients, trig_table, twist_cos, twist_sin):
    waves_all = coefficients.shape[-1]
    weights = jnp.where(jnp.arange(waves_all) == 0, 1.0, 2.0).astype(jnp.bfloat16)
    scaled = coefficients * weights
    leading = scaled.shape[:3] + (waves_all // SUBW, SUBW)
    stacked = jnp.concatenate(
        [scaled[:, :, :, 0].reshape(leading), scaled[:, :, :, 1].reshape(leading)], axis=4
    )
    partial_h = jnp.einsum(
        "rflqj,rkj->rflqk", stacked, trig_table, preferred_element_type=jnp.float32
    )
    row_points = twist_cos.shape[-1]
    return jnp.sum(
        twist_cos[:, None, None] * partial_h[..., :row_points]
        - twist_sin[:, None, None] * partial_h[..., row_points:],
        axis=3,
    )


def analyze(weighted, trig_table, twist_cos, twist_sin):
    spread = weighted[:, :, :, None, :]
    turned = jnp.concatenate(
        [spread * twist_cos[:, None, None], -(spread * twist_sin[:, None, None])], axis=4
    ).astype(jnp.bfloat16)
    result = jnp.einsum("rflqk,rkj->rflqj", turned, trig_table, preferred_element_type=jnp.float32)
    leading = result.shape[:3] + (result.shape[3] * SUBW,)
    weights = jnp.where(jnp.arange(leading[3]) == 0, 1.0, 2.0)
    return jnp.stack(
        [
            result[..., :SUBW].reshape(leading) * weights,
            result[..., SUBW:].reshape(leading) * weights,
        ],
        axis=3,
    ).astype(jnp.bfloat16)


def body(spec_in, observation_weight, latitude_row_length, wave_map, row_map):
    band_count = lax.axis_size("band")
    level_groups = lax.axis_size("lev")
    owners = band_count * level_groups
    owner_index = lax.axis_index("band") * level_groups + lax.axis_index("lev")
    columns = spec_in.shape[4]
    truncation = columns - 2
    waves_all = truncation + 1
    blocks = waves_all // SUBW
    row_cap = observation_weight.shape[0]
    level_count = observation_weight.shape[1]
    row_points = observation_weight.shape[2]
    row_total = latitude_row_length.shape[0]
    pair_dev = spec_in.shape[3] // level_groups
    spectra = lax.all_to_all(spec_in, "lev", split_axis=3, concat_axis=2, tiled=True)
    cos_lat, log_sin = latitudes(latitude_row_length, (row_points - 16) // 4)
    pair_ids = lax.dynamic_slice_in_dim(wave_map, owner_index * pair_dev, pair_dev)
    functions = legendre(pair_ids, cos_lat, log_sin, truncation).astype(jnp.bfloat16)
    side_sel = side_mask(pair_ids, truncation).astype(jnp.bfloat16)
    masked = spectra[..., None] * side_sel
    fourier = jnp.einsum(
        "qnr,filqns->rfliqs", functions, masked, preferred_element_type=jnp.float32
    ).astype(jnp.bfloat16)
    slot_of_row, chosen = slot_table(row_map, owners, row_cap)
    picker = chosen.astype(jnp.bfloat16)
    outgoing = jnp.dot(
        picker, fourier.reshape(row_total, -1), preferred_element_type=jnp.float32
    ).astype(jnp.bfloat16)
    outgoing = outgoing.reshape(owners, row_cap, 2, level_count, 2, 2 * pair_dev)
    arrived = lax.all_to_all(outgoing, ("band", "lev"), split_axis=0, concat_axis=0, tiled=True)
    m_of_w, w_of_m = wave_order(wave_map, truncation)
    coefficients = jnp.transpose(arrived, (1, 2, 3, 4, 0, 5)).reshape(
        row_cap, 2, level_count, 2, waves_all
    )
    coefficients = jnp.take(coefficients, w_of_m, axis=4)
    slot_length = jnp.sum(jnp.where(chosen, latitude_row_length[None, :], 0), axis=1)
    my_length = lax.dynamic_slice_in_dim(slot_length, owner_index * row_cap, row_cap)
    trig_table, twist_cos, twist_sin = fourier_tables(my_length, row_points, blocks)
    grid_incr = synthesize(coefficients, trig_table, twist_cos, twist_sin)
    weighted = grid_incr * observation_weight[:, None].astype(jnp.float32)
    back = analyze(weighted, trig_table, twist_cos, twist_sin)
    back = jnp.take(back, m_of_w, axis=4).reshape(row_cap, 2, level_count, 2, owners, 2 * pair_dev)
    returning = jnp.transpose(back, (4, 0, 1, 2, 3, 5))
    returned = lax.all_to_all(returning, ("band", "lev"), split_axis=0, concat_axis=0, tiled=True)
    by_row = jnp.dot(
        picker.T, returned.reshape(owners * row_cap, -1), preferred_element_type=jnp.float32
    ).astype(jnp.bfloat16)
    by_row = by_row.reshape(row_total, 2, level_count, 2, pair_dev, 2)
    normaliser = 1.0 / math.sqrt(row_total * row_points)
    gradient = jnp.einsum(
        "qnr,rfliqs->filqns", functions, by_row, preferred_element_type=jnp.float32
    )
    gradient = (jnp.sum(gradient * side_sel, axis=5) * normaliser).astype(jnp.bfloat16)
    spec_grad = lax.all_to_all(gradient, "lev", split_axis=2, concat_axis=3, tiled=True)
    return (grid_incr, spec_grad)


def solution(mesh):
    return jax.shard_map(
        body,
        mesh=mesh,
        in_specs=(
            P("member", None, "lev", "band", None),
            P(("band", "lev"), "member", None),
            P(),
            P(),
            P(),
        ),
        out_specs=(
            P(("band", "lev"), None, "member", None),
            P("member", None, "lev", "band", None),
        ),
        check_vma=False,
    )
```

profile of v0, /device:TPU:0, one launch (start us, length us, event | category | flops | bytes accessed | tf_op | source)
XLA Modules:
  0.0 1022.7 jit_solution(2671748276966209701)
XLA Ops:
  0.6 4.1 copy.97
  4.7 6.3 all-to-all-start
  16.1 5.5 scatter_custom_fusion
  27.0 735.1 %while.17 = (s32[]{:T(128)}, f32[40,16]{0,1:T(8,128)S(1)}, f32[40,16]{0,1:T(8,128)S(1)}, bf16[80,16,40,16]{2,3,1,0:T(8,128)(2,1)}, pred[80,16,40]{2,1,0:T(8,128)...) while((s32[]{:T(128)}, f32[40,16]{0,1:T(8,128)S(1)}, ...), condition=%wide.region_6.7_spmd.clone.clone.clone, body=%wide.region_5.6_spmd.clone.clone.clone.sunk | while | flops 197777 | bytes 717143 | solution.py:74
  82.9 1.6 fusion.238
  92.1 1.6 fusion.238
  110.5 1.6 fusion.238
  119.6 1.6 fusion.238
  202.3 1.6 fusion.238
  229.8 1.6 fusion.238
  275.7 1.6 fusion.238
  284.9 1.6 fusion.238
  294.1 1.6 fusion.238
  321.7 1.6 fusion.238
  358.4 1.6 fusion.238
  367.6 1.6 fusion.238
  404.3 1.9 fusion.238
  441.2 1.6 fusion.238
  477.9 1.6 fusion.238
  505.5 1.6 fusion.238
  560.6 1.6 fusion.238
  569.8 1.9 fusion.238
  579.2 1.6 fusion.238
  634.2 1.6 fusion.238
  652.6 1.6 fusion.238
  716.9 1.6 fusion.238
  765.0 10.2 %fusion.132 = (f32[2,10,5136]{2,1,0:T(8,128)S(1)}, f32[2,10,5136]{2,1,0:T(8,128)}) fusion(f32[2]{0:T(128)} %convert_divide_fusion, s32[2]{0:T(128)} %get-tuple-element.302, s32[10,5136]{1,0:T(8,128)S(1)} %iota_multiply_fusion.1), kind=kLoop, calls=%fused_computation.240 | loop fusion | flops 821760 | bytes 1027216 | tf_op jit(solution)/shard_map/cos | solution.py:116
  778.1 8.5 copy.100
  786.8 82.2 %negate_convert_fusion.1 = (bf16[2,5136,128]{2,1,0:T(8,128)(2,1)}, bf16[2,5136,128]{2,1,0:T(8,128)(2,1)}, bf16[2,5136,128]{2,1,0:T(8,128)(2,1)}) fusion(f32[2]{0:T(128)S(1)} %copy-done.19, s32[2]{0:T(128)S(1)} %copy-done.15, s32[5136,128]{1,0:T(8,128)S(1)} %iota_multiply_fusion, pred[2,5136]{1,0:T(4,128)(4,1)S(1)} %iota_compare_fusion.3), kind=kLoop, calls=%fused_computation.212 | loop fusion | flops 18407424 | bytes 10528816 | tf_op jit(solution)/shard_map/convert.9
  870.5 2.5 fusion.126
  874.5 6.1 all-to-all-start.1
  880.7 7.3 all-to-all-done.1
  888.6 4.2 copy.121
  892.8 9.3 gather_fusion
  902.2 9.0 bitcast_multiply_fusion.1
  911.2 4.7 fusion.232
  915.9 4.8 copy.105
  921.4 3.0 copy.106
  924.5 6.3 fusion.103
  930.8 2.1 fusion.105
  936.3 2.6 fusion.102
  939.2 2.1 copy.109
  941.3 9.3 gather_fusion.1
  950.6 6.4 broadcast_select_fusion.1
  956.9 2.2 copy.110
  959.2 10.4 %all_to_all.31 = bf16[16,2,2,4,2,80]{5,4,3,2,1,0:T(2,128)(2,1)S(1)} all-to-all(bf16[16,2,2,4,2,80]{5,4,3,2,1,0:T(2,128)(2,1)S(1)} %bitcast.300), channel_id=1, replica_groups=mesh['member'=2,'band'=4,'lev'=4] {'band','lev'}, dimensions={0} | all-to-all | bytes 163840 | tf_op jit(solution)/shard_map/all_to_all | solution.py:198
  970.2 4.7 fusion.101
  976.3 44.9 %all_to_all.32 = bf16[2,2,4,40,1281]{4,3,1,0,2:T(8,128)(2,1)S(1)} all-to-all(bf16[2,2,4,40,1281]{4,3,1,0,2:T(8,128)(2,1)S(1)} %copy.114), channel_id=1, replica_groups=mesh['member'=2,'band'=4,'lev'=4] {'lev'}, dimensions={2} | all-to-all | bytes 3279360 | tf_op jit(solution)/shard_map/all_to_all | solution.py:208
  (1693 shorter events, 724.3 us)
Async XLA Ops:
  0.6 10.5 %copy-start.14 = (s32[640]{0:T(1024)S(1)}, s32[640]{0:T(1024)}, u32[]{:S(2)}) copy-start(s32[640]{0:T(1024)} %param.12) | copy-start | bytes 7684
  4.7 864.3 %all-to-all-start = ((bf16[2,2,1,160,1281]{4,1,2,0,3:T(2,128)(2,1)}), bf16[2,2,1,160,1281]{4,1,2,0,3:T(2,128)(2,1)S(1)}, u32[]{:S(2)}, u32[]{:S(2)}) async-start(bf16[2,2,1,160,1281]{4,1,2,0,3:T(2,128)(2,1)} %copy.97), calls=%async_computation | async-start | bytes 3604480 | tf_op jit(solution)/shard_map/all_to_all | solution.py:169
  11.1 11.7 %copy-start.20 = (s32[16]{0:T(128)S(1)}, s32[16]{0:T(128)}, u32[]{:S(2)}) copy-start(s32[16]{0:T(128)} %param.11) | copy-start | bytes 196
  11.1 11.7 %copy-start.18 = (s32[16]{0:T(128)S(1)}, s32[16]{0:T(128)}, u32[]{:S(2)}) copy-start(s32[16]{0:T(128)} %param.13) | copy-start | bytes 196
  23.1 3.7 copy-start.16
  778.1 91.9 %copy-start.8 = (bf16[1,40,16]{0,2,1:T(8,128)(2,1)}, bf16[1,40,16]{0,2,1:T(8,128)(2,1)S(1)}, u32[]{:S(2)}) copy-start(bf16[1,40,16]{0,2,1:T(8,128)(2,1)S(1)} %copy.101) | copy-start | bytes 3844
  778.1 8.7 copy-start.15
  778.1 8.7 copy-start.19
  869.1 1.4 copy-start.4
  870.5 2.8 copy-start.17
  870.5 10.1 copy-start.10
  873.0 19.8 %copy-start.12 = (s32[2048]{0:T(1024)S(1)}, s32[2048]{0:T(1024)}, u32[]{:S(2)}) copy-start(s32[2048]{0:T(1024)} %pad_clamp_fusion.1) | copy-start | bytes 24580
  873.0 29.1 %copy-start.13 = (pred[1280]{0:T(1024)(128)(4,1)S(1)}, pred[1280]{0:T(1024)(128)(4,1)}, u32[]{:S(2)}) copy-start(pred[1280]{0:T(1024)(128)(4,1)} %compare_and_fusion.1) | copy-start | bytes 3844
  874.5 13.5 %all-to-all-start.1 = ((bf16[16,2,2,4,2,80]{5,4,3,2,1,0:T(2,128)(2,1)}), bf16[16,2,2,4,2,80]{5,4,3,2,1,0:T(2,128)(2,1)S(1)}, u32[]{:S(2)}, u32[]{:S(2)}) async-start(bf16[16,2,2,4,2,80]{5,4,3,2,1,0:T(2,128)(2,1)} %reshape.768), calls=%async_computation.1 | async-start | bytes 262144 | tf_op jit(solution)/shard_map/all_to_all | solution.py:184
  888.0 0.7 copy-start.6
  924.5 6.3 copy-start
  932.9 0.9 copy-start.5
  932.9 1.9 copy-start.3
  933.0 2.6 copy-start.1
  933.0 3.3 copy-start.2
  936.3 2.7 copy-start.11
  950.6 19.6 %copy-start.7 = (f32[40,1281,2]{1,2,0:T(2,128)S(1)}, f32[40,1281,2]{1,2,0:T(2,128)}, u32[]{:S(2)}) copy-start(f32[40,1281,2]{1,2,0:T(2,128)} %get-tuple-element.296) | copy-start | bytes 1229764
  950.6 19.6 %copy-start.9 = (bf16[1,40,16]{0,2,1:T(8,128)(2,1)S(1)}, bf16[1,40,16]{0,2,1:T(8,128)(2,1)}, u32[]{:S(2)}) copy-start(bf16[1,40,16]{0,2,1:T(8,128)(2,1)} %copy-done.8) | copy-start | bytes 3844
where the time goes:
time: 1030 us; the launch traced here: 1020 us
  other arithmetic  676 us (66%)
  local copies, waits for them, and re-layouts  251 us (24%)
  blocking collectives  55.3 us (5%)
  matrix products  16.6 us (2%)
  starting transfers between devices  12.4 us (1%)
    while x1200, other arithmetic  441 us
    mul x81, local copies, waits for them, and re-layouts, advance(): lagged_c[:, None] * oldest  131 us
    another operation x3, other arithmetic  83 us
    or x80, other arithmetic, advance(): fresh = first_c[:, None] | second_c[:, None]  52.6 us
    select_n x80, other arithmetic, advance(): oldest = jnp.where(fresh, 0.0, older)  51.2 us
    dynamic_update_slice x80, local copies, waits for them, and re-layouts, legendre(): _, values = lax.scan(advance, (empty, empty), packed, unroll=16)  50.3 us
    all_to_all x1, blocking collectives, body(): lax.all_to_all(gradient, 'lev', split_axis=2, concat_axis=3, tiled=True)  44.9 us
  transfers between devices with their start and end apart: 2, of which 1 were waited for; matrix products, arithmetic and copies ran while one was open for 84% of the time, Pallas kernels for 0%

commit v1 on v0

v1 whole, which is shorter than its diff:
```python
import math

import jax
import jax.numpy as jnp
from jax import lax
from jax.experimental import pallas as pl
from jax.experimental.pallas import tpu as pltpu
from jax.sharding import PartitionSpec as P

SUBW = 128
LANES = 128
CHUNK = 144


def latitudes(latitude_row_length, halves):
    cycle_no = ((latitude_row_length - 16) // 4).astype(jnp.float32)
    colat = math.pi * (cycle_no - 0.25) / (2.0 * halves + 0.5)
    north = (
        jnp.arange(latitude_row_length.shape[0], dtype=jnp.int32)
        < latitude_row_length.shape[0] // 2
    )
    return (jnp.where(north, jnp.cos(colat), -jnp.cos(colat)), jnp.log(jnp.sin(colat)))


def diagonals(pair_ids, log_sin, truncation):
    first_order = pair_ids[:, None]
    counter = jnp.arange(1, truncation + 1, dtype=jnp.int32)
    log_terms = jnp.log(1.0 - 0.5 / counter.astype(jnp.float32))

    def start(orders):
        partial_sum = jnp.sum(
            jnp.where(counter[None, :] <= orders, log_terms[None, :], 0.0), axis=1, keepdims=True
        )
        order_m = orders.astype(jnp.float32)
        log_start = 0.5 * (jnp.log(order_m + 0.5) + partial_sum)
        return jnp.exp(log_start + order_m * log_sin[None, :])

    return (start(first_order), start(truncation - first_order))


def legendre_kernel(
    truncation, groups, group_pad, blocks, part, ids, spread, mu, diag1, diag2, bound, out,
    slopes, laggeds, values, newer, older,
):
    step = pl.program_id(0)
    half = groups // blocks

    @pl.when(step == 0)
    def _():
        newer[...] = jnp.zeros_like(newer)
        older[...] = diag1[...]

    column = lax.broadcasted_iota(jnp.int32, (CHUNK, 256), 0) + step * CHUNK
    lane = lax.broadcasted_iota(jnp.int32, (CHUNK, 256), 1)

    def split(x):
        high = x.astype(jnp.bfloat16).astype(jnp.float32)
        rest = x - high
        middle = rest.astype(jnp.bfloat16).astype(jnp.float32)
        low = rest - middle
        piece = jnp.where(lane < part, high, jnp.where(lane < 2 * part, middle, low))
        return piece.astype(jnp.bfloat16)

    for b in range(blocks):
        first_order = ids[b : b + 1, :]
        boundary = truncation + 1 - first_order
        first_side = column < boundary
        order_m = jnp.where(first_side, first_order, truncation - first_order).astype(jnp.float32)
        degree = jnp.where(first_side, first_order + column, column - 1).astype(jnp.float32)
        restart_first = column == 0
        restart = restart_first | (column == boundary)

        def epsilon(v):
            upper = jnp.maximum(v * v - order_m * order_m, 0.0)
            lower = jnp.maximum(4.0 * v * v - 1.0, 1.0)
            return jnp.sqrt(upper / lower)

        inverse = 1.0 / jnp.where(restart, 1.0, epsilon(degree))
        slope = jnp.where(restart, 0.0, inverse)
        lagged = jnp.where(restart, 0.0, -epsilon(degree - 1.0) * inverse)
        lagged = jnp.where(restart_first, 1.0, lagged)
        for table, compact in ((slopes, slope), (laggeds, lagged)):
            wide = jnp.dot(split(compact), spread[...], preferred_element_type=jnp.float32)
            for g in range(half):
                table[pl.ds(b * half + g, CHUNK, stride=group_pad), :] = wide[
                    :, g * LANES : (g + 1) * LANES
                ]

    mu_v = mu[...]
    diag2_v = diag2[...]
    bound_v = bound[...]

    def advance(i, carry):
        new, old = carry
        rows = pl.ds(pl.multiple_of(i * group_pad, 8), group_pad)
        lag = jnp.where(bound_v == step * CHUNK + i, diag2_v, laggeds[rows, :] * old)
        value = slopes[rows, :] * mu_v * new + lag
        values[rows, :] = value
        return (value, new)

    new, old = lax.fori_loop(0, CHUNK, advance, (newer[...], older[...]), unroll=16)
    newer[...] = new
    older[...] = old
    for g in range(groups):
        out[g] = values[pl.ds(g, CHUNK, stride=group_pad), :].astype(jnp.bfloat16)


def legendre(pair_ids, cos_lat, log_sin, truncation):
    pairs = pair_ids.shape[0]
    rows = cos_lat.shape[0]
    groups = pairs * rows // LANES
    group_pad = -(-groups // 8) * 8
    blocks = -(-pairs // 80)
    part = pairs // blocks
    chunks = -(-(truncation + 2) // CHUNK)
    diag1, diag2 = diagonals(pair_ids, log_sin, truncation)

    def lay(x):
        x = jnp.broadcast_to(x, (pairs, rows)).reshape(groups, LANES)
        return jnp.pad(x, ((0, group_pad - groups), (0, 0)))

    ids = jnp.tile(pair_ids.reshape(blocks, part), (1, 3))
    ids = jnp.pad(ids, ((0, 0), (0, 256 - 3 * part)))
    source = jnp.arange(256, dtype=jnp.int32)[:, None]
    target = jnp.arange(part * rows, dtype=jnp.int32)[None, :] // rows
    spread = ((source % part == target) & (source < 3 * part)).astype(jnp.bfloat16)
    whole = pl.BlockSpec(memory_space=pltpu.VMEM)
    tall = pltpu.VMEM((CHUNK * group_pad, LANES), jnp.float32)
    state = pltpu.VMEM((group_pad, LANES), jnp.float32)

    def kernel(*refs):
        legendre_kernel(truncation, groups, group_pad, blocks, part, *refs)

    return pl.pallas_call(
        kernel,
        grid=(chunks,),
        in_specs=[whole] * 6,
        out_specs=pl.BlockSpec((groups, CHUNK, LANES), lambda i: (0, i, 0)),
        out_shape=jax.ShapeDtypeStruct((groups, chunks * CHUNK, LANES), jnp.bfloat16),
        scratch_shapes=[tall, tall, tall, state, state],
        compiler_params=pltpu.CompilerParams(vmem_limit_bytes=48 * 2**20),
        name="legendre",
    )(
        ids,
        spread,
        lay(cos_lat[None, :]),
        lay(diag1),
        lay(diag2),
        lay(truncation + 1 - pair_ids[:, None]),
    )


def slot_table(row_map, owners, row_cap):
    onehot = (row_map[:, None] == jnp.arange(owners, dtype=jnp.int32)[None, :]).astype(jnp.int32)
    ranking = jnp.sum((jnp.cumsum(onehot, axis=0) - onehot) * onehot, axis=1)
    slot_of_row = row_map * row_cap + ranking
    return slot_of_row[None, :] == jnp.arange(owners * row_cap, dtype=jnp.int32)[:, None]


def angle_tables(lengths, orders, points):
    safe_len = jnp.maximum(lengths, 1)[:, None, None]
    step_angle = 2.0 * math.pi / safe_len.astype(jnp.float32)
    angles = (points[None, :, None] * orders[None, None, :] % safe_len).astype(
        jnp.float32
    ) * step_angle
    return jnp.cos(angles), jnp.sin(angles)


def fourier_tables(lengths, high_count, blocks):
    low = jnp.arange(LANES, dtype=jnp.int32)
    high = jnp.arange(high_count, dtype=jnp.int32) * LANES
    inner = jnp.arange(SUBW, dtype=jnp.int32)
    outer = jnp.arange(blocks, dtype=jnp.int32) * SUBW
    slots = lengths.shape[0]
    low_c, low_s = (x[:, None] for x in angle_tables(lengths, inner, low))
    high_c, high_s = (x[:, :, None] for x in angle_tables(lengths, inner, high))
    shape = (slots, high_count * LANES, SUBW)
    cosine = (low_c * high_c - low_s * high_s).astype(jnp.bfloat16).reshape(shape)
    sine = (low_s * high_c + low_c * high_s).astype(jnp.bfloat16).reshape(shape)
    low_c, low_s = (x[:, :, None] for x in angle_tables(lengths, low, outer))
    high_c, high_s = (x[:, :, :, None] for x in angle_tables(lengths, high, outer))
    shape = (slots, blocks, high_count * LANES)
    twist_cos = (low_c * high_c - low_s * high_s).reshape(shape)
    twist_sin = (low_s * high_c + low_c * high_s).reshape(shape)
    return cosine, sine, twist_cos, twist_sin


def body(spec_in, observation_weight, latitude_row_length, wave_map, row_map):
    bands = lax.axis_size("band")
    levels = lax.axis_size("lev")
    owners = bands * levels
    owner_index = lax.axis_index("band") * levels + lax.axis_index("lev")
    columns = spec_in.shape[4]
    truncation = columns - 2
    waves_all = truncation + 1
    blocks = waves_all // SUBW
    row_cap = observation_weight.shape[0]
    row_points = observation_weight.shape[2]
    rows = latitude_row_length.shape[0]
    pairs = spec_in.shape[3]
    grouped = LANES // rows
    groups = pairs // grouped
    cos_lat, log_sin = latitudes(latitude_row_length, (row_points - 16) // 4)
    pair_ids = lax.dynamic_slice_in_dim(wave_map, lax.axis_index("band") * pairs, pairs)
    functions = legendre(pair_ids, cos_lat, log_sin, truncation)[:, :columns]
    own = jnp.eye(grouped, dtype=jnp.float32)[None, None, None, None, :, :, None]

    first_side = (
        jnp.arange(columns, dtype=jnp.int32)[None, :] < truncation + 1 - pair_ids[:, None]
    )
    sides = jnp.stack([first_side, jnp.logical_not(first_side)]).astype(jnp.bfloat16)
    masked = spec_in[None, :, :, 0] * sides[:, None, None]
    masked = masked.reshape(2, 2, 2, groups, grouped, columns)
    product = jnp.einsum(
        "gnx,sfigcn->gsficx", functions, masked, preferred_element_type=jnp.float32
    )
    product = product.reshape(groups, 2, 2, 2, grouped, grouped, rows)
    fourier = jnp.sum(product * own, axis=5).astype(jnp.bfloat16)
    fourier = jnp.transpose(fourier, (5, 2, 3, 0, 4, 1)).reshape(rows, -1)

    chosen = slot_table(row_map, owners, row_cap)
    picker = chosen.astype(jnp.bfloat16)
    outgoing = jnp.dot(picker, fourier, preferred_element_type=jnp.float32).astype(jnp.bfloat16)
    outgoing = outgoing.reshape(owners, row_cap * 4, 2 * pairs)
    arrived = lax.all_to_all(outgoing, ("band", "lev"), split_axis=0, concat_axis=0, tiled=True)
    arrived = arrived.reshape(bands, levels, row_cap, 2, 2, 2 * pairs)
    arrived = jnp.transpose(arrived, (2, 3, 1, 4, 0, 5)).reshape(-1, waves_all)
    doubled = jnp.repeat(wave_map, 2)
    odd = jnp.arange(waves_all, dtype=jnp.int32) % 2
    m_of_w = jnp.where(odd == 0, doubled, truncation - doubled)
    order = jnp.arange(waves_all, dtype=jnp.int32)
    gain = jnp.where(order == 0, 1.0, 2.0)
    permute = jnp.where(m_of_w[:, None] == order[None, :], gain[None, :], 0.0).astype(jnp.bfloat16)
    scaled = jnp.dot(arrived, permute, preferred_element_type=jnp.float32).astype(jnp.bfloat16)
    scaled = scaled.reshape(row_cap, 2, levels, 2, blocks, SUBW)

    slot_length = jnp.sum(jnp.where(chosen, latitude_row_length[None, :], 0), axis=1)
    lengths = lax.dynamic_slice_in_dim(slot_length, owner_index * row_cap, row_cap)
    high_count = -(-row_points // LANES)
    cosine, sine, twist_cos, twist_sin = fourier_tables(lengths, high_count, blocks)
    stacked = jnp.concatenate([scaled[:, :, :, 0], scaled[:, :, :, 1]], axis=4)
    table_re = jnp.concatenate([cosine, -sine], axis=2)
    table_im = jnp.concatenate([sine, cosine], axis=2)
    half_re = jnp.einsum("rflqj,rkj->rflqk", stacked, table_re, preferred_element_type=jnp.float32)
    half_im = jnp.einsum("rflqj,rkj->rflqk", stacked, table_im, preferred_element_type=jnp.float32)
    spread_cos = twist_cos[:, None, None]
    spread_sin = twist_sin[:, None, None]
    grid = jnp.sum(spread_cos * half_re - spread_sin * half_im, axis=3)
    inside = jnp.arange(high_count * LANES, dtype=jnp.int32)[None, :] < lengths[:, None]
    grid = jnp.where(inside[:, None, None], grid, 0.0)
    grid_incr = grid[..., :row_points]

    weight = jnp.pad(
        observation_weight.astype(jnp.float32), ((0, 0), (0, 0), (0, high_count * LANES - row_points))
    )
    weighted = (grid * weight[:, None])[:, :, :, None]
    turned_re = (weighted * spread_cos).astype(jnp.bfloat16)
    turned_im = (-(weighted * spread_sin)).astype(jnp.bfloat16)
    result = jnp.einsum(
        "rflqk,rkj->rflqj", turned_re, table_re, preferred_element_type=jnp.float32
    ) + jnp.einsum("rflqk,rkj->rflqj", turned_im, table_im, preferred_element_type=jnp.float32)
    back = jnp.stack([result[..., :SUBW], result[..., SUBW:]], axis=3).astype(jnp.bfloat16)
    back = back.reshape(-1, waves_all)
    back = lax.dot_general(
        back, permute, (((1,), (1,)), ((), ())), preferred_element_type=jnp.float32
    ).astype(jnp.bfloat16)
    back = back.reshape(row_cap, 2, levels, 2, bands, 2 * pairs)
    returning = jnp.transpose(back, (4, 2, 0, 1, 3, 5)).reshape(owners, row_cap * 4, 2 * pairs)
    returned = lax.all_to_all(returning, ("band", "lev"), split_axis=0, concat_axis=0, tiled=True)
    by_row = jnp.dot(
        picker.T, returned.reshape(owners * row_cap, -1), preferred_element_type=jnp.float32
    ).astype(jnp.bfloat16)
    by_row = by_row.reshape(rows, 2, 2, groups, grouped, 2)
    by_row = jnp.transpose(by_row, (3, 5, 1, 2, 4, 0))[:, :, :, :, :, None]
    spread_rows = (by_row * own.astype(jnp.bfloat16)).reshape(groups, 2, 2, 2, grouped, LANES)
    gradient = jnp.einsum(
        "gsficx,gnx->sfigcn", spread_rows, functions, preferred_element_type=jnp.float32
    ).reshape(2, 2, 2, pairs, columns)
    normaliser = 1.0 / math.sqrt(rows * row_points)
    gradient = jnp.where(first_side, gradient[0], gradient[1]) * normaliser
    return (grid_incr, gradient.astype(jnp.bfloat16)[:, :, None])


def solution(mesh):
    return jax.shard_map(
        body,
        mesh=mesh,
        in_specs=(
            P("member", None, "lev", "band", None),
            P(("band", "lev"), "member", None),
            P(),
            P(),
            P(),
        ),
        out_specs=(
            P(("band", "lev"), None, "member", None),
            P("member", None, "lev", "band", None),
        ),
        check_vma=False,
    )
```

time: 1030 us -> 99.5 us (0.10)
  other arithmetic: 676 us -> 20.9 us
  local copies, waits for them, and re-layouts: 251 us -> 18.7 us
  blocking collectives: 55.3 us -> 0 us
  Pallas kernels: 0 us -> 16.5 us
    while x1200 -> x0, other arithmetic: 441 us -> none
    mul x82 -> x12, local copies, waits for them, and re-layouts: 132 us -> 6.52 us  [the longest x4 5.91 us: body(): by_row * own.astype(jnp.bfloat16)]
    another operation x4 -> x1, other arithmetic: 83.1 us -> 0.03 us  [body(): jnp.stack([result[..., :SUBW], result[..., SUBW:]], axis=3)]
    select_n x86 -> x5, other arithmetic: 60.6 us -> 0.7 us  [the longest x1 0.61 us: body(): m_of_w = jnp.where(odd == 0, doubled, truncation - doubled)]
    all_to_all x2 -> x0, blocking collectives: 55.3 us -> none  [the longest x1 44.9 us: body(): lax.all_to_all(gradient, 'lev', split_axis=2, concat_axis=3, tiled=True)]
    or x80 -> x0, other arithmetic: 52.6 us -> none  [advance(): fresh = first_c[:, None] | second_c[:, None]]
    dynamic_update_slice x80 -> x0, local copies, waits for them, and re-layouts: 50.3 us -> none  [legendre(): _, values = lax.scan(advance, (empty, empty), packed, unroll=16)]
    gather x2 -> x0, local copies, waits for them, and re-layouts: 18.6 us -> none  [the longest x1 9.3 us: body(): coefficients = jnp.take(coefficients, w_of_m, axis=4)]
  transfers between devices with their start and end apart: 2 -> 2, of which waited for: 1 -> 1; matrix products, arithmetic and copies ran while one was open for 84% -> 13% of each run, Pallas kernels for 0% -> 0%
where the time goes in v1:
time: 99.5 us; the launch traced here: 99 us
  matrix products  21.6 us (22%)
  other arithmetic  20.9 us (21%)
  local copies, waits for them, and re-layouts  18.7 us (19%)
  Pallas kernels  16.5 us (17%)
  starting transfers between devices  13.4 us (13%)
  waiting for transfers between devices  6.63 us (7%)
  between operations  1.26 us (1%)
    pallas_call x1, Pallas kernels, legendre(): pl.pallas_call(kernel, grid=(chunks,), in_specs=[whole] * 6, out_specs=pl...  16.5 us
    all_to_all x1, starting transfers between devices, body(): lax.all_to_all(outgoing, ('band', 'lev'), split_axis=0, concat_axis=0, ti...  7.41 us
    all_to_all x1, waiting for transfers between devices, body(): lax.all_to_all(returning, ('band', 'lev'), split_axis=0, concat_axis=0, t...  6.62 us
    all_to_all x1, starting transfers between devices, body(): lax.all_to_all(returning, ('band', 'lev'), split_axis=0, concat_axis=0, t...  5.94 us
    mul x4, local copies, waits for them, and re-layouts, body(): by_row * own.astype(jnp.bfloat16)  5.91 us
    dot_general x1, matrix products, body(): jnp.einsum('gsficx,gnx->sfigcn', spread_rows, functions, preferred_elemen...  5.08 us
    dot_general x1, matrix products, body(): jnp.einsum('gnx,sfigcn->gsficx', functions, masked, preferred_element_typ...  4.77 us
    reduce_sum x1, other arithmetic, body(): fourier = jnp.sum(product * own, axis=5).astype(jnp.bfloat16)  4.27 us
  transfers between devices with their start and end apart: 2, of which 1 were waited for; matrix products, arithmetic and copies ran while one was open for 13% of the time, Pallas kernels for 0%

profile of v1, /device:TPU:0, one launch (start us, length us, event | category | flops | bytes accessed | tf_op | source)
XLA Modules:
  0.0 99.0 jit_solution(2287647588148187063)
XLA Ops:
  0.7 0.9 broadcast_subtract_fusion.1
  1.7 0.3 select_reduce_fusion
  3.1 0.7 sine_log_fusion
  4.2 0.3 iota_compare_fusion.2
  4.9 0.3 and_convert_fusion.refs_1_
  5.2 16.5 %legendre.1 = bf16[20,1296,128]{2,1,0:T(8,128)(2,1)} custom-call(s32[2,256]{1,0:T(2,128)S(1)} %pad.25.refs_0_, bf16[256,1280]{1,0:T(8,128)(2,1)S(1)} %and_convert_fusion.refs_1_, f32[24,128]{1,0:T(8,128)S(1)} %pad.26.refs_2_, f32[24,128]{1,0:T(8,128)S(1)} %pad.27.refs_3_, f32[24,128]{1,0:T(8,128)S(1)} %pad.28.refs_4_, s32[24,128]{1,0:T(8,128)S(1)} %pad.29.refs_5_), custom_call_target="tpu_custom_call" | custom-call | tf_op jit(solution)/shard_map/legendre/pallas_call | solution.py:134
  21.7 4.8 %fusion.2 = f32[20,2,2,2,8,128]{5,4,3,2,1,0:T(8,128)S(1)} fusion(bf16[20,1296,128]{2,1,0:T(8,128)(2,1)} %legendre.1, bf16[2,20,8,1281]{3,2,0,1:T(8,128)(2,1)S(1)} %add_convert_fusion.1, bf16[2,2,1,160,1281]{4,3,2,1,0:T(8,128)(2,1)S(1)} %copy-done), kind=kOutput, calls=%fused_computation.14 | convolution fusion | flops 426316800 | bytes 9709440 | tf_op jit(solution)/shard_map/gnx,sfigcn->gsficx/dot_general | solution.py:214
  26.5 3.1 %reshape.551 = f32[20,2,2,2,8,8,16]{6,5,4,3,2,1,0:T(8,128)} reshape(f32[20,2,2,2,8,128]{5,4,3,2,1,0:T(8,128)S(1)} %fusion.2) | data formatting | bytes 1310720 | tf_op jit(solution)/shard_map/reshape | solution.py:217
  29.6 4.3 %multiply_reduce_fusion = bf16[20,2,2,2,8,16]{5,4,3,2,1,0:T(8,128)(2,1)S(1)} fusion(f32[20,2,2,2,8,8,16]{6,5,4,3,2,1,0:T(8,128)} %reshape.551, f32[8,8]{1,0:T(8,128)S(1)} %fusion.60), kind=kLoop, calls=%fused_computation.12 | loop fusion | flops 307200 | bytes 696576 | tf_op jit(solution)/shard_map/reduce_sum | solution.py:218
  33.9 0.3 copy.52
  34.2 0.2 select_reduce_fusion.3
  34.4 0.3 convolution_convert_fusion
  34.7 0.8 reshape.553
  35.6 7.4 %all-to-all-start = ((bf16[16,8,320]{2,1,0:T(8,128)(2,1)}), bf16[16,8,320]{2,1,0:T(8,128)(2,1)}, u32[]{:S(2)}, u32[]{:S(2)}) async-start(bf16[16,8,320]{2,1,0:T(8,128)(2,1)} %reshape.553), calls=%async_computation | async-start | bytes 196608 | tf_op jit(solution)/shard_map/all_to_all | solution.py:225
  43.4 0.7 iota_compare_fusion.3
  44.3 0.2 reshape.556
  44.5 0.7 fusion.63
  45.2 0.7 fusion.65
  45.8 0.8 fusion.41
  46.6 1.8 %fusion.34 = (f32[2,128,128]{2,1,0:T(8,128)S(1)}, f32[2,128,128]{2,1,0:T(8,128)S(1)}) fusion(f32[2]{0:T(128)S(1)} %convert_divide_fusion, s32[2]{0:T(128)S(1)} %get-tuple-element.18, s32[128,128]{1,0:T(8,128)S(1)} %iota_multiply_fusion), kind=kLoop, calls=%fused_computation.64 | loop fusion | flops 262144 | bytes 327696 | tf_op jit(solution)/shard_map/cos | solution.py:166
  48.4 2.9 %add_convert_fusion = (bf16[2,41,128,128]{3,2,1,0:T(8,128)(2,1)S(1)}, bf16[2,41,128,128]{3,2,1,0:T(8,128)(2,1)}) fusion(f32[2,41,128]{2,1,0:T(8,128)S(1)} %get-tuple-element.33, f32[2,128,128]{2,1,0:T(8,128)S(1)} %get-tuple-element.29, f32[2,41,128]{2,1,0:T(8,128)S(1)} %get-tuple-element.32, f32[2,128,128]{2,1,0:T(8,128)S(1)} %get-tuple-element.28), kind=kLoop, calls=%fused_computation.10 | loop fusion | flops 10747904 | bytes 5720064 | tf_op jit(solution)/shard_map/convert_element_type | solution.py:179
  51.3 1.6 %copy-done.1 = bf16[2,41,128,128]{3,2,1,0:T(8,128)(2,1)} copy-done((bf16[2,41,128,128]{3,2,1,0:T(8,128)(2,1)}, bf16[2,41,128,128]{3,2,1,0:T(8,128)(2,1)S(1)}, u32[]{:S(2)}) %copy-start.1) | copy-done | bytes 2687000
  52.9 2.1 %bitcast_negate_fusion = bf16[2,5248,128]{2,1,0:T(8,128)(2,1)} fusion(bf16[2,41,128,128]{3,2,1,0:T(8,128)(2,1)S(1)} %get-tuple-element.22), kind=kLoop, calls=%fused_computation.153 | loop fusion | flops 1343488 | bytes 5373952 | tf_op jit(solution)/shard_map/neg | solution.py:242
  55.0 0.3 multiply_subtract_fusion
  55.3 0.6 subtract_select_fusion
  55.9 0.2 add.227
  56.2 0.2 sub.73
  56.5 0.9 copy.50
  57.4 0.9 reshape.554
  58.5 1.5 %fusion.21 = bf16[32,1280]{1,0:T(8,128)(2,1)S(1)} fusion(bf16[32,1280]{1,0:T(8,128)(2,1)S(1)} %reshape.555, bf16[1280]{0:T(1024)(128)(2,1)S(1)} %fusion.55, s32[1280]{0:T(1024)} %subtract_select_fusion), kind=kOutput, calls=%fused_computation.34 | convolution fusion | flops 108175360 | bytes 171520 | tf_op jit(solution)/shard_map/dot_general | solution.py:234
  60.1 3.9 %convolution_multiply_fusion = f32[2,2,4,10,5248]{4,3,2,1,0:T(8,128)S(1)} fusion(bf16[2,5248,128]{2,1,0:T(8,128)(2,1)} %bitcast.92, bf16[2,5248,128]{2,1,0:T(8,128)(2,1)} %bitcast.90, f32[2,10,5248]{2,1,0:T(8,128)S(1)} %copy.56, bf16[2,2,4,10,128]{4,3,2,1,0:T(8,128)(2,1)S(1)} %get-tuple-element.27, bf16[2,2,4,10,128]{4,3,2,1,0:T(8,128)(2,1)S(1)} %get-tuple-element.26), kind=kOutput, calls=%fused_computation | convolution fusion | flops 441667584 | bytes 9234432 | tf_op jit(solution)/shard_map/rflqj,rkj->rflqk/dot_general | solution.py:245
  64.1 0.2 copy-done.4
  64.4 2.3 %fusion.23 = f32[2,2,4,5248]{3,2,1,0:T(4,128)S(1)} fusion(f32[2,2,4,10,5248]{4,3,2,1,0:T(8,128)S(1)} %convolution_multiply_fusion, bf16[2,5248,128]{2,1,0:T(8,128)(2,1)S(1)} %copy-done.4, bf16[2,5248,128]{2,1,0:T(8,128)(2,1)S(1)} %bitcast.93, f32[2,10,5248]{2,1,0:T(8,128)S(1)} %copy-done.5, bf16[2,2,4,10,128]{4,3,2,1,0:T(8,128)(2,1)S(1)} %get-tuple-element.27, ...), kind=kOutput, calls=%fused_computation.38 | convolution fusion | flops 443262976 | bytes 9570304 | tf_op jit(solution)/shard_map/rflqj,rkj->rflqk/dot_general | solution.py:244
  66.8 0.9 broadcast_multiply_fusion
  67.6 1.1 %fusion.9 = f32[2,2,4,10,256]{4,3,2,1,0:T(8,128)S(1)} fusion(bf16[2,5248,128]{2,1,0:T(8,128)(2,1)S(1)} %bitcast.94, bf16[2,5248,128]{2,1,0:T(8,128)(2,1)S(1)} %bitcast.91, f32[2,2,4,5248]{3,2,1,0:T(4,128)S(1)} %get-tuple-element.12, f32[2,10,5248]{2,1,0:T(8,128)S(1)} %copy.56), kind=kOutput, calls=%fused_computation.22 | convolution fusion | flops 443183104 | bytes 6293504 | tf_op jit(solution)/shard_map/rflqk,rkj->rflqj/dot_general | solution.py:261
  68.8 1.2 %fusion.28 = bf16[2,2,4,10,256]{4,3,2,1,0:T(8,128)(2,1)S(1)} fusion(f32[2,2,4,10,256]{4,3,2,1,0:T(8,128)S(1)} %fusion.9, bf16[2,5248,128]{2,1,0:T(8,128)(2,1)S(1)} %copy-done.4, bf16[2,5248,128]{2,1,0:T(8,128)(2,1)S(1)} %bitcast.95, f32[2,2,4,5248]{3,2,1,0:T(4,128)S(1)} %get-tuple-element.12, f32[2,10,5248]{2,1,0:T(8,128)S(1)} %copy-done.5), kind=kOutput, calls=%fused_computation.45 | convolution fusion | flops 442425344 | bytes 6375424 | tf_op jit(solution)/shard_map/rflqk,rkj->rflqj/dot_general | solution.py:259
  70.1 1.2 %fusion.22 = bf16[32,1280]{1,0:T(8,128)(2,1)S(1)} fusion(bf16[1280]{0:T(1024)(128)(2,1)S(1)} %fusion.55, s32[1280]{0:T(1024)S(1)} %copy-done.10, bf16[4,8,10,128]{3,2,1,0:T(8,128)(2,1)S(1)} %bitcast.102), kind=kOutput, calls=%fused_computation.35 | convolution fusion | flops 108175360 | bytes 171520 | tf_op jit(solution)/shard_map/dot_general | solution.py:264
  71.6 0.7 reshape.559
  72.3 5.9 %all-to-all-start.1 = ((bf16[16,8,320]{2,1,0:T(8,128)(2,1)}), bf16[16,8,320]{2,1,0:T(8,128)(2,1)S(1)}, u32[]{:S(2)}, u32[]{:S(2)}) async-start(bf16[16,8,320]{2,1,0:T(8,128)(2,1)} %reshape.559), calls=%async_computation.1 | async-start | bytes 196608 | tf_op jit(solution)/shard_map/all_to_all | solution.py:269
  78.2 0.2 iota_compare_fusion.1
  78.6 6.6 %all-to-all-done.1 = bf16[16,8,320]{2,1,0:T(8,128)(2,1)S(1)} async-done(((bf16[16,8,320]{2,1,0:T(8,128)(2,1)}), bf16[16,8,320]{2,1,0:T(8,128)(2,1)S(1)}, u32[]{:S(2)}, u32[]{:S(2)}) %all-to-all-start.1) | async-done | bytes 81952 | tf_op jit(solution)/shard_map/all_to_all | solution.py:269
  85.4 0.2 convolution_convert_fusion.1
  85.6 0.2 copy.59
  85.9 2.2 %mul.512 = bf16[20,2,2,2,8,8,16]{6,5,4,3,2,1,0:T(8,128)(2,1)} broadcast(bf16[20,2,2,2,8,16]{5,4,3,2,1,0:T(8,128)(2,1)S(1)} %copy.60), dimensions={0,1,2,3,4,6} | broadcast | bytes 368640 | tf_op jit(solution)/shard_map/mul | solution.py:275
  88.2 3.5 %mul.513 = bf16[20,2,2,2,8,128]{5,4,3,2,1,0:T(8,128)(2,1)S(1)} reshape(bf16[20,2,2,2,8,8,16]{6,5,4,3,2,1,0:T(8,128)(2,1)} %mul.512) | data formatting | bytes 655360 | tf_op jit(solution)/shard_map/mul | solution.py:275
  91.7 5.1 %fusion.3 = f32[2,2,2,20,8,1281]{5,4,2,1,0,3:T(8,128)S(1)} fusion(bf16[20,1296,128]{2,1,0:T(8,128)(2,1)} %legendre.1, bf16[20,2,2,2,8,128]{5,4,3,2,1,0:T(8,128)(2,1)S(1)} %mul.513, bf16[8,128]{1,0:T(8,128)(2,1)S(1)} %mul.515), kind=kOutput, calls=%fused_computation.15 | convolution fusion | flops 420413440 | bytes 13483008 | tf_op jit(solution)/shard_map/gsficx,gnx->sfigcn/dot_general | solution.py:276
  96.7 0.6 fusion.74
  97.3 1.7 %fusion.24 = bf16[2,2,1,160,1281]{4,3,2,1,0:T(8,128)(2,1)} fusion(f32[1,2,2,20,8,1281]{5,4,2,1,0,3:T(8,128)S(1)} %get-tuple-element.21, f32[1,2,2,20,8,1281]{5,4,2,1,0,3:T(8,128)S(1)} %get-tuple-element.20, pred[160,1281]{1,0:T(8,128)(4,1)S(1)} %iota_compare_fusion.1), kind=kLoop, calls=%fused_computation.39 | loop fusion | flops 2459520 | bytes 8403360
  (100 shorter events, 3.8 us)
Async XLA Ops:
  0.6 21.0 %copy-start = (bf16[2,2,1,160,1281]{4,3,2,1,0:T(8,128)(2,1)S(1)}, bf16[2,2,1,160,1281]{4,3,2,1,0:T(8,128)(2,1)}, u32[]{:S(2)}) copy-start(bf16[2,2,1,160,1281]{4,3,2,1,0:T(8,128)(2,1)} %param.5) | copy-start | bytes 4919044
  1.6 3.6 %copy-start.8 = (s32[160]{0:T(256)}, s32[160]{0:T(256)S(1)}, u32[]{:S(2)}) copy-start(s32[160]{0:T(256)S(1)} %get-tuple-element.14) | copy-start | bytes 1924
  26.4 7.7 %copy-start.14 = (s32[16]{0:T(128)S(1)}, s32[16]{0:T(128)}, u32[]{:S(2)}) copy-start(s32[16]{0:T(128)} %param.9) | copy-start | bytes 196
  26.5 16.5 %copy-start.15 = (s32[16]{0:T(128)S(1)}, s32[16]{0:T(128)}, u32[]{:S(2)}) copy-start(s32[16]{0:T(128)} %param.7) | copy-start | bytes 196
  26.5 17.7 %copy-start.11 = (s32[640]{0:T(1024)S(1)}, s32[640]{0:T(1024)}, u32[]{:S(2)}) copy-start(s32[640]{0:T(1024)} %param.8) | copy-start | bytes 7684
  34.4 8.7 %copy-start.12 = (s32[16]{0:T(128)}, s32[16]{0:T(128)S(1)}, u32[]{:S(2)}) copy-start(s32[16]{0:T(128)S(1)} %multiply_add_fusion.1) | copy-start | bytes 196
  35.6 21.8 %all-to-all-start = ((bf16[16,8,320]{2,1,0:T(8,128)(2,1)}), bf16[16,8,320]{2,1,0:T(8,128)(2,1)}, u32[]{:S(2)}, u32[]{:S(2)}) async-start(bf16[16,8,320]{2,1,0:T(8,128)(2,1)} %reshape.553), calls=%async_computation | async-start | bytes 196608 | tf_op jit(solution)/shard_map/all_to_all | solution.py:225
  48.4 6.6 %copy-start.6 = (bf16[2,4,5136]{2,1,0:T(4,128)(2,1)S(1)}, bf16[2,4,5136]{2,1,0:T(4,128)(2,1)}, u32[]{:S(2)}) copy-start(bf16[2,4,5136]{2,1,0:T(4,128)(2,1)} %param.6) | copy-start | bytes 246532
  51.3 1.6 %copy-start.1 = (bf16[2,41,128,128]{3,2,1,0:T(8,128)(2,1)}, bf16[2,41,128,128]{3,2,1,0:T(8,128)(2,1)S(1)}, u32[]{:S(2)}) copy-start(bf16[2,41,128,128]{3,2,1,0:T(8,128)(2,1)S(1)} %get-tuple-element.22) | copy-start | bytes 8060932
  60.1 4.0 %copy-start.3 = (bf16[2,41,128,128]{3,2,1,0:T(8,128)(2,1)S(1)}, bf16[2,41,128,128]{3,2,1,0:T(8,128)(2,1)}, u32[]{:S(2)}) copy-start(bf16[2,41,128,128]{3,2,1,0:T(8,128)(2,1)} %get-tuple-element.23) | copy-start | bytes 8060932
  60.1 4.2 %copy-start.4 = (bf16[2,5248,128]{2,1,0:T(8,128)(2,1)S(1)}, bf16[2,5248,128]{2,1,0:T(8,128)(2,1)}, u32[]{:S(2)}) copy-start(bf16[2,5248,128]{2,1,0:T(8,128)(2,1)} %bitcast_negate_fusion) | copy-start | bytes 8060932
  60.1 4.3 %copy-start.5 = (f32[2,10,5248]{2,1,0:T(8,128)S(1)}, f32[2,10,5248]{2,1,0:T(8,128)}, u32[]{:S(2)}) copy-start(f32[2,10,5248]{2,1,0:T(8,128)} %copy.50) | copy-start | bytes 1259524
  64.4 2.3 %copy-start.7 = (pred[2,5248]{1,0:T(4,128)(4,1)S(1)}, pred[2,5248]{1,0:T(4,128)(4,1)}, u32[]{:S(2)}) copy-start(pred[2,5248]{1,0:T(4,128)(4,1)} %iota_compare_fusion.3) | copy-start | bytes 31492
  64.4 3.2 %copy-start.2 = (bf16[2,41,128,128]{3,2,1,0:T(8,128)(2,1)S(1)}, bf16[2,41,128,128]{3,2,1,0:T(8,128)(2,1)}, u32[]{:S(2)}) copy-start(bf16[2,41,128,128]{3,2,1,0:T(8,128)(2,1)} %copy-done.1) | copy-start | bytes 8060932
  68.8 1.3 %copy-start.10 = (s32[1280]{0:T(1024)S(1)}, s32[1280]{0:T(1024)}, u32[]{:S(2)}) copy-start(s32[1280]{0:T(1024)} %subtract_select_fusion) | copy-start | bytes 15364
  70.0 8.2 %copy-start.9 = (s32[160]{0:T(256)S(1)}, s32[160]{0:T(256)}, u32[]{:S(2)}) copy-start(s32[160]{0:T(256)} %copy-done.8) | copy-start | bytes 1924
  70.0 15.4 %copy-start.13 = (s32[16]{0:T(128)S(1)}, s32[16]{0:T(128)}, u32[]{:S(2)}) copy-start(s32[16]{0:T(128)} %copy-done.12) | copy-start | bytes 196
  72.3 13.0 %all-to-all-start.1 = ((bf16[16,8,320]{2,1,0:T(8,128)(2,1)}), bf16[16,8,320]{2,1,0:T(8,128)(2,1)S(1)}, u32[]{:S(2)}, u32[]{:S(2)}) async-start(bf16[16,8,320]{2,1,0:T(8,128)(2,1)} %reshape.559), calls=%async_computation.1 | async-start | bytes 196608 | tf_op jit(solution)/shard_map/all_to_all | solution.py:269

commit v2 on v1

--- a/solution.py
+++ b/solution.py
@@ -39,11 +39,13 @@
 
 
 def legendre_kernel(
-    truncation, groups, group_pad, blocks, part, ids, spread, mu, diag1, diag2, bound, out,
-    slopes, laggeds, values, newer, older,
+    truncation, groups, group_pad, blocks, part, cluster, ids, spread, mu, diag1, diag2, bound,
+    limit, own, spec, out, fourier, slopes, laggeds, values, newer, older, kept,
 ):
     step = pl.program_id(0)
     half = groups // blocks
+    wide_lanes = kept.shape[2]
+    tiles = wide_lanes // LANES
 
     @pl.when(step == 0)
     def _():
@@ -70,14 +72,14 @@
         restart_first = column == 0
         restart = restart_first | (column == boundary)
 
-        def epsilon(v):
+        def squared(v):
             upper = jnp.maximum(v * v - order_m * order_m, 0.0)
             lower = jnp.maximum(4.0 * v * v - 1.0, 1.0)
-            return jnp.sqrt(upper / lower)
-
-        inverse = 1.0 / jnp.where(restart, 1.0, epsilon(degree))
+            return upper / lower
+
+        inverse = lax.rsqrt(jnp.where(restart, 1.0, squared(degree)))
         slope = jnp.where(restart, 0.0, inverse)
-        lagged = jnp.where(restart, 0.0, -epsilon(degree - 1.0) * inverse)
+        lagged = jnp.where(restart, 0.0, -jnp.sqrt(squared(degree - 1.0)) * inverse)
         lagged = jnp.where(restart_first, 1.0, lagged)
         for table, compact in ((slopes, slope), (laggeds, lagged)):
             wide = jnp.dot(split(compact), spread[...], preferred_element_type=jnp.float32)
@@ -101,17 +103,71 @@
     new, old = lax.fori_loop(0, CHUNK, advance, (newer[...], older[...]), unroll=16)
     newer[...] = new
     older[...] = old
+    here = pl.ds(pl.multiple_of(step * CHUNK, CHUNK), CHUNK)
     for g in range(groups):
-        out[g] = values[pl.ds(g, CHUNK, stride=group_pad), :].astype(jnp.bfloat16)
-
-
-def legendre(pair_ids, cos_lat, log_sin, truncation):
+        piece = values[pl.ds(g, CHUNK, stride=group_pad), :].astype(jnp.bfloat16)
+        lanes = pl.ds((g % tiles) * LANES, LANES)
+        out[g // tiles, :, lanes] = piece
+        kept[g // tiles, here, lanes] = piece
+
+    @pl.when(step == pl.num_programs(0) - 1)
+    def _():
+        columns = spec.shape[3]
+        point = lax.broadcasted_iota(jnp.int32, (cluster, columns), 1)
+        for k in range(groups // tiles):
+            pairs = pl.ds(k * cluster, cluster)
+            first = jnp.where(point < limit[pairs, :], 1.0, 0.0).astype(jnp.bfloat16)
+            table = kept[k, :columns, :]
+            operands = []
+            for f in range(2):
+                for i in range(2):
+                    x = spec[f, i, pairs, :]
+                    y = x * first
+                    operands += [y, x - y]
+            product = jnp.dot(
+                jnp.concatenate(operands, axis=0), table, preferred_element_type=jnp.float32
+            )
+            product = product.reshape(8, cluster, wide_lanes) * own[...][None]
+            fourier[k] = jnp.sum(product, axis=1)
+
+
+def adjoint_kernel(cluster, normaliser, limit, own, back, table, out):
+    columns = out.shape[3]
+    mask = own[...]
+    rows = back[0]
+    operands = [mask * rows[x : x + 1, :] for x in range(8)]
+    result = lax.dot_general(
+        jnp.concatenate(operands, axis=0).astype(jnp.bfloat16),
+        table[0],
+        (((1,), (1,)), ((), ())),
+        preferred_element_type=jnp.float32,
+    )
+    first = lax.broadcasted_iota(jnp.int32, (cluster, columns), 1) < limit[...]
+    for x in range(4):
+        one = result[2 * x * cluster : (2 * x + 1) * cluster, :columns]
+        two = result[(2 * x + 1) * cluster : (2 * x + 2) * cluster, :columns]
+        out[x // 2, x % 2] = (jnp.where(first, one, two) * normaliser).astype(jnp.bfloat16)
+
+
+def cluster_of(pairs):
+    return 16 if pairs % 16 == 0 else pairs
+
+
+def own_mask(cluster, rows):
+    lane = jnp.arange(cluster * rows, dtype=jnp.int32)[None, :] // rows
+    return (lane == jnp.arange(cluster, dtype=jnp.int32)[:, None]).astype(jnp.float32)
+
+
+def legendre(spec, pair_ids, cos_lat, log_sin, truncation):
     pairs = pair_ids.shape[0]
     rows = cos_lat.shape[0]
     groups = pairs * rows // LANES
     group_pad = -(-groups // 8) * 8
     blocks = -(-pairs // 80)
     part = pairs // blocks
+    cluster = cluster_of(pairs)
+    clusters = pairs // cluster
+    wide = cluster * rows
     chunks = -(-(truncation + 2) // CHUNK)
     diag1, diag2 = diagonals(pair_ids, log_sin, truncation)
 
@@ -127,27 +183,55 @@
     whole = pl.BlockSpec(memory_space=pltpu.VMEM)
     tall = pltpu.VMEM((CHUNK * group_pad, LANES), jnp.float32)
     state = pltpu.VMEM((group_pad, LANES), jnp.float32)
+    limit = truncation + 1 - pair_ids[:, None]
 
     def kernel(*refs):
-        legendre_kernel(truncation, groups, group_pad, blocks, part, *refs)
+        legendre_kernel(truncation, groups, group_pad, blocks, part, cluster, *refs)
 
     return pl.pallas_call(
         kernel,
         grid=(chunks,),
-        in_specs=[whole] * 6,
-        out_specs=pl.BlockSpec((groups, CHUNK, LANES), lambda i: (0, i, 0)),
-        out_shape=jax.ShapeDtypeStruct((groups, chunks * CHUNK, LANES), jnp.bfloat16),
-        scratch_shapes=[tall, tall, tall, state, state],
-        compiler_params=pltpu.CompilerParams(vmem_limit_bytes=48 * 2**20),
+        in_specs=[whole] * 9,
+        out_specs=(pl.BlockSpec((clusters, CHUNK, wide), lambda i: (0, i, 0)), whole),
+        out_shape=(
+            jax.ShapeDtypeStruct((clusters, chunks * CHUNK, wide), jnp.bfloat16),
+            jax.ShapeDtypeStruct((clusters, 8, wide), jnp.float32),
+        ),
+        scratch_shapes=[
+            tall, tall, tall, state, state,
+            pltpu.VMEM((clusters, chunks * CHUNK, wide), jnp.bfloat16),
+        ],
+        compiler_params=pltpu.CompilerParams(vmem_limit_bytes=58 * 2**20),
         name="legendre",
     )(
-        ids,
-        spread,
-        lay(cos_lat[None, :]),
-        lay(diag1),
-        lay(diag2),
-        lay(truncation + 1 - pair_ids[:, None]),
-    )
+        ids, spread, lay(cos_lat[None, :]), lay(diag1), lay(diag2), lay(limit), limit,
+        own_mask(cluster, rows), spec,
+    )
+
+
+def adjoint(back, table, pair_ids, rows, columns, normaliser):
+    pairs = pair_ids.shape[0]
+    cluster = cluster_of(pairs)
+    wide = cluster * rows
+    limit = columns - 1 - pair_ids[:, None]
+
+    def kernel(*refs):
+        adjoint_kernel(cluster, normaliser, *refs)
+
+    return pl.pallas_call(
+        kernel,
+        grid=(pairs // cluster,),
+        in_specs=[
+            pl.BlockSpec((cluster, 1), lambda i: (i, 0)),
+            pl.BlockSpec((cluster, wide), lambda i: (0, 0)),
+            pl.BlockSpec((1, 8, wide), lambda i: (i, 0, 0)),
+            pl.BlockSpec((1, table.shape[1], wide), lambda i: (i, 0, 0)),
+        ],
+        out_specs=pl.BlockSpec((2, 2, cluster, columns), lambda i: (0, 0, i, 0)),
+        out_shape=jax.ShapeDtypeStruct((2, 2, pairs, columns), jnp.bfloat16),
+        compiler_params=pltpu.CompilerParams(vmem_limit_bytes=58 * 2**20),
+        name="adjoint",
+    )(limit, own_mask(cluster, rows), back, table)
 
 
 def slot_table(row_map, owners, row_cap):
@@ -198,25 +282,13 @@
     row_points = observation_weight.shape[2]
     rows = latitude_row_length.shape[0]
     pairs = spec_in.shape[3]
-    grouped = LANES // rows
-    groups = pairs // grouped
     cos_lat, log_sin = latitudes(latitude_row_length, (row_points - 16) // 4)
     pair_ids = lax.dynamic_slice_in_dim(wave_map, lax.axis_index("band") * pairs, pairs)
-    functions = legendre(pair_ids, cos_lat, log_sin, truncation)[:, :columns]
-    own = jnp.eye(grouped, dtype=jnp.float32)[None, None, None, None, :, :, None]
-
-    first_side = (
-        jnp.arange(columns, dtype=jnp.int32)[None, :] < truncation + 1 - pair_ids[:, None]
-    )
-    sides = jnp.stack([first_side, jnp.logical_not(first_side)]).astype(jnp.bfloat16)
-    masked = spec_in[None, :, :, 0] * sides[:, None, None]
-    masked = masked.reshape(2, 2, 2, groups, grouped, columns)
-    product = jnp.einsum(
-        "gnx,sfigcn->gsficx", functions, masked, preferred_element_type=jnp.float32
-    )
-    product = product.reshape(groups, 2, 2, 2, grouped, grouped, rows)
-    fourier = jnp.sum(product * own, axis=5).astype(jnp.bfloat16)
-    fourier = jnp.transpose(fourier, (5, 2, 3, 0, 4, 1)).reshape(rows, -1)
+    functions, fourier = legendre(spec_in[:, :, 0], pair_ids, cos_lat, log_sin, truncation)
+    clusters = functions.shape[0]
+    cluster = pairs // clusters
+    fourier = fourier.astype(jnp.bfloat16).reshape(clusters, 2, 2, 2, cluster, rows)
+    fourier = jnp.transpose(fourier, (5, 1, 2, 0, 4, 3)).reshape(rows, -1)
 
     chosen = slot_table(row_map, owners, row_cap)
     picker = chosen.astype(jnp.bfloat16)
@@ -270,15 +342,13 @@
     by_row = jnp.dot(
         picker.T, returned.reshape(owners * row_cap, -1), preferred_element_type=jnp.float32
     ).astype(jnp.bfloat16)
-    by_row = by_row.reshape(rows, 2, 2, groups, grouped, 2)
-    by_row = jnp.transpose(by_row, (3, 5, 1, 2, 4, 0))[:, :, :, :, :, None]
-    spread_rows = (by_row * own.astype(jnp.bfloat16)).reshape(groups, 2, 2, 2, grouped, LANES)
-    gradient = jnp.einsum(
-        "gsficx,gnx->sfigcn", spread_rows, functions, preferred_element_type=jnp.float32
-    ).reshape(2, 2, 2, pairs, columns)
+    by_row = by_row.reshape(rows, 2, 2, clusters, cluster, 2)
+    by_row = jnp.transpose(by_row, (3, 1, 2, 5, 4, 0)).reshape(clusters, 8, cluster * rows)
     normaliser = 1.0 / math.sqrt(rows * row_points)
-    gradient = jnp.where(first_side, gradient[0], gradient[1]) * normaliser
-    return (grid_incr, gradient.astype(jnp.bfloat16)[:, :, None])
+    gradient = adjoint(
+        by_row.astype(jnp.float32), functions, pair_ids, rows, columns, normaliser
+    )
+    return (grid_incr, gradient[:, :, None])
 
 
 def solution(mesh):

time: 99.5 us -> 104 us (1.045)
  Pallas kernels: 16.5 us -> 30.4 us
  blocking collectives: 0 us -> 12.8 us
  matrix products: 21.6 us -> 12.2 us
  waiting for transfers between devices: 6.63 us -> 0.01 us
  starting transfers between devices: 13.4 us -> 7.34 us
  other arithmetic: 20.9 us -> 16.8 us
  local copies, waits for them, and re-layouts: 18.7 us -> 22.1 us
    pallas_call x1 -> x2, Pallas kernels: 16.5 us -> 30.4 us  [the longest x1 21 us: legendre(): pl.pallas_call(kernel, grid=(chunks,), in_specs=[whole] * 9, out_specs=(p...]
    all_to_all x0 -> x1, blocking collectives: none -> 12.8 us  [body(): lax.all_to_all(returning, ('band', 'lev'), split_axis=0, concat_axis=0, t...]
    dot_general x2 -> x0, matrix products: 9.84 us -> none  [the longest x1 5.08 us: body(): jnp.einsum('gsficx,gnx->sfigcn', spread_rows, functions, preferred_elemen...]
    all_to_all x1 -> x0, waiting for transfers between devices: 6.62 us -> none  [body(): lax.all_to_all(returning, ('band', 'lev'), split_axis=0, concat_axis=0, t...]
    all_to_all x1 -> x0, starting transfers between devices: 5.94 us -> none  [body(): lax.all_to_all(returning, ('band', 'lev'), split_axis=0, concat_axis=0, t...]
    mul x4 -> x0, local copies, waits for them, and re-layouts: 5.91 us -> none  [body(): by_row * own.astype(jnp.bfloat16)]
    reduce_sum x1 -> x0, other arithmetic: 4.27 us -> none  [body(): fourier = jnp.sum(product * own, axis=5).astype(jnp.bfloat16)]
    sub x2, local copies, waits for them, and re-layouts: 1.13 us -> 3.93 us  [fourier_tables(): twist_cos = (low_c * high_c - low_s * high_s).reshape(shape)]
  transfers between devices with their start and end apart: 2 -> 1, of which waited for: 1 -> 0; matrix products, arithmetic and copies ran while one was open for 13% -> 17% of each run, Pallas kernels for 0% -> 0%
where the time goes in v2:
time: 104 us; the launch traced here: 103 us
  Pallas kernels  30.4 us (29%)
  local copies, waits for them, and re-layouts  22.1 us (21%)
  other arithmetic  16.8 us (16%)
  blocking collectives  12.8 us (12%)
  matrix products  12.2 us (12%)
  starting transfers between devices  7.34 us (7%)
  between operations  1.1 us (1%)
    pallas_call x1, Pallas kernels, legendre(): pl.pallas_call(kernel, grid=(chunks,), in_specs=[whole] * 9, out_specs=(p...  21 us
    all_to_all x1, blocking collectives, body(): lax.all_to_all(returning, ('band', 'lev'), split_axis=0, concat_axis=0, t...  12.8 us
    pallas_call x1, Pallas kernels, adjoint(): pl.pallas_call(kernel, grid=(pairs // cluster,), in_specs=[pl.BlockSpec((...  9.32 us
    all_to_all x1, starting transfers between devices, body(): lax.all_to_all(outgoing, ('band', 'lev'), split_axis=0, concat_axis=0, ti...  7.34 us
    sub x2, local copies, waits for them, and re-layouts, fourier_tables(): twist_cos = (low_c * high_c - low_s * high_s).reshape(shape)  3.93 us
    cos x4, other arithmetic, angle_tables(): return (jnp.cos(angles), jnp.sin(angles))  3.9 us
    dot_general x1, matrix products, body(): jnp.einsum('rflqj,rkj->rflqk', stacked, table_im, preferred_element_type=...  3.53 us
    convert_element_type x1, other arithmetic, fourier_tables(): sine = (low_s * high_c + low_c * high_s).astype(jnp.bfloat16).reshape(shape)  2.95 us
  transfers between devices with their start and end apart: 1, of which 0 were waited for; matrix products, arithmetic and copies ran while one was open for 17% of the time, Pallas kernels for 0%

profile of v2, /device:TPU:0, one launch (start us, length us, event | category | flops | bytes accessed | tf_op | source)
XLA Modules:
  0.0 102.7 jit_solution(4703669328293119994)
XLA Ops:
  0.7 0.8 broadcast_subtract_fusion
  1.6 0.3 select_reduce_fusion
  3.0 0.7 sine_log_fusion
  3.8 0.6 pad.27.refs_3_
  4.5 0.6 pad.28.refs_4_
  5.1 0.6 pad.25.refs_0_
  5.8 0.8 copy.37.refs_6_.refs_0_
  6.7 0.6 pad.29.refs_5_
  7.5 0.6 pad.26.refs_2_
  8.1 0.6 fusion.33.refs_7_.refs_1_
  8.7 1.1 %and_convert_fusion.refs_1_ = bf16[256,1280]{1,0:T(8,128)(2,1)} fusion(s32[1280]{0:T(1024)S(1)} %add_select_fusion.1, s32[256]{0:T(256)S(1)} %and_select_fusion.4, pred[256]{0:T(512)(128)(4,1)S(1)} %iota_compare_fusion.7), kind=kLoop, calls=%fused_computation.31 | loop fusion | flops 983040 | bytes 661760 | tf_op jit(solution)/shard_map/convert_element_type | solution.py:182
  9.8 21.0 %legendre.1 = (bf16[10,1296,256]{2,1,0:T(8,128)(2,1)}, f32[10,8,256]{2,1,0:T(8,128)}) custom-call(s32[2,256]{1,0:T(2,128)} %pad.25.refs_0_, bf16[256,1280]{1,0:T(8,128)(2,1)} %and_convert_fusion.refs_1_, f32[24,128]{1,0:T(8,128)} %pad.26.refs_2_, f32[24,128]{1,0:T(8,128)} %pad.27.refs_3_, f32[24,128]{1,0:T(8,128)} %pad.28.refs_4_, s32[24,128]{1,0:T(8,128)} %pad.29.refs_5_, ...), custom_call_target="tpu_custom_call" | custom-call | tf_op jit(solution)/shard_map/legendre/pallas_call | solution.py:191
  30.8 0.9 convert_element_type.149
  31.7 0.3 reshape.473
  32.0 0.3 copy.38
  32.6 0.3 convolution_convert_fusion
  32.9 0.8 reshape.475
  33.7 7.3 %all-to-all-start = ((bf16[16,8,320]{2,1,0:T(8,128)(2,1)}), bf16[16,8,320]{2,1,0:T(8,128)(2,1)}, u32[]{:S(2)}, u32[]{:S(2)}) async-start(bf16[16,8,320]{2,1,0:T(8,128)(2,1)} %reshape.475), calls=%async_computation | async-start | bytes 196608 | tf_op jit(solution)/shard_map/all_to_all | solution.py:297
  41.7 0.2 reshape.478
  42.0 0.7 fusion.52
  42.6 0.7 fusion.54
  43.3 0.8 fusion.31
  44.0 1.8 %fusion.24 = (f32[2,128,128]{2,1,0:T(8,128)S(1)}, f32[2,128,128]{2,1,0:T(8,128)S(1)}) fusion(f32[2]{0:T(128)S(1)} %convert_divide_fusion, s32[2]{0:T(128)S(1)} %get-tuple-element.22, s32[128,128]{1,0:T(8,128)S(1)} %iota_multiply_fusion), kind=kLoop, calls=%fused_computation.47 | loop fusion | flops 262144 | bytes 327696 | tf_op jit(solution)/shard_map/cos | solution.py:250
  45.9 2.9 %add_convert_fusion = (bf16[2,41,128,128]{3,2,1,0:T(8,128)(2,1)S(1)}, bf16[2,41,128,128]{3,2,1,0:T(8,128)(2,1)}) fusion(f32[2,41,128]{2,1,0:T(8,128)S(1)} %get-tuple-element.35, f32[2,128,128]{2,1,0:T(8,128)S(1)} %get-tuple-element.31, f32[2,41,128]{2,1,0:T(8,128)S(1)} %get-tuple-element.34, f32[2,128,128]{2,1,0:T(8,128)S(1)} %get-tuple-element.30), kind=kLoop, calls=%fused_computation.9 | loop fusion | flops 10747904 | bytes 5720064 | tf_op jit(solution)/shard_map/convert_element_type | solution.py:263
  48.8 2.0 %bitcast_negate_fusion = bf16[2,5248,128]{2,1,0:T(8,128)(2,1)} fusion(bf16[2,41,128,128]{3,2,1,0:T(8,128)(2,1)S(1)} %get-tuple-element.24), kind=kLoop, calls=%fused_computation.139 | loop fusion | flops 1343488 | bytes 5373952 | tf_op jit(solution)/shard_map/neg | solution.py:314
  50.9 1.1 %multiply_subtract_fusion = (f32[2,10,41,128]{3,2,0,1:T(8,128)}, f32[2,10,41,128]{3,2,0,1:T(8,128)S(1)}) fusion(f32[2,10,41]{2,0,1:T(2,128)S(1)} %get-tuple-element.39, f32[2,10,128]{2,0,1:T(2,128)S(1)} %get-tuple-element.37, f32[2,10,41]{2,0,1:T(2,128)S(1)} %get-tuple-element.38, f32[2,10,128]{2,0,1:T(2,128)S(1)} %get-tuple-element.36), kind=kLoop, calls=%fused_computation.37 | loop fusion | flops 629760 | bytes 866720 | tf_op jit(solution)/shard_map/sub | solution.py:267
  52.0 0.6 subtract_select_fusion
  52.6 1.0 add.233
  53.6 1.1 %copy.42 = f32[2,10,5248]{2,1,0:T(8,128)S(1)} copy(f32[2,10,5248]{2,0,1:T(2,128)} %add.233) | data formatting | bytes 839680 | tf_op jit(solution)/shard_map/add | solution.py:268
  54.6 2.0 %sub.84 = f32[2,10,5248]{2,0,1:T(2,128)} reshape(f32[2,10,41,128]{3,2,0,1:T(8,128)} %get-tuple-element.32) | data formatting | bytes 839680 | tf_op jit(solution)/shard_map/sub | solution.py:267
  56.7 1.9 %copy.36 = f32[2,10,5248]{2,1,0:T(8,128)} copy(f32[2,10,5248]{2,0,1:T(2,128)} %sub.84) | data formatting | bytes 839680 | tf_op jit(solution)/shard_map/sub | solution.py:267
  58.6 1.6 %reshape.476 = bf16[4,4,2,2,2,320]{5,4,3,2,1,0:T(2,128)(2,1)} reshape(bf16[16,8,320]{2,1,0:T(8,128)(2,1)} %all-to-all-done) | data formatting | bytes 163840 | tf_op jit(solution)/shard_map/reshape | solution.py:298
  60.2 1.6 %copy.39 = bf16[2,2,4,2,4,320]{5,4,3,2,1,0:T(4,128)(2,1)} copy(bf16[2,2,4,2,4,320]{5,3,1,0,2,4:T(2,128)(2,1)} %bitcast.73) | data formatting | bytes 163840 | tf_op jit(solution)/shard_map/transpose | solution.py:299
  61.7 1.7 %reshape.477 = bf16[32,1280]{1,0:T(8,128)(2,1)} reshape(bf16[2,2,4,2,4,320]{5,4,3,2,1,0:T(4,128)(2,1)} %copy.39) | data formatting | bytes 163840 | tf_op jit(solution)/shard_map/reshape | solution.py:299
  63.4 2.4 %fusion.15 = bf16[32,1280]{1,0:T(8,128)(2,1)} fusion(bf16[32,1280]{1,0:T(8,128)(2,1)} %reshape.477, bf16[1280]{0:T(1024)(128)(2,1)S(1)} %fusion.46, s32[1280]{0:T(1024)} %subtract_select_fusion), kind=kOutput, calls=%fused_computation.25 | convolution fusion | flops 108175360 | bytes 171520 | tf_op jit(solution)/shard_map/dot_general | solution.py:306
  65.8 1.6 %reshape.479 = bf16[2,2,4,2,10,128]{5,4,3,2,1,0:T(8,128)(2,1)} reshape(bf16[32,1280]{1,0:T(8,128)(2,1)} %fusion.15) | data formatting | bytes 163840 | tf_op jit(solution)/shard_map/reshape | solution.py:307
  67.4 0.9 slice_bitcast_fusion.3
  68.3 3.5 %convolution_multiply_fusion = f32[2,2,4,10,5248]{4,3,2,1,0:T(8,128)S(1)} fusion(bf16[2,5248,128]{2,1,0:T(8,128)(2,1)} %bitcast.65, bf16[2,5248,128]{2,1,0:T(8,128)(2,1)S(1)} %bitcast.63, f32[2,10,5248]{2,1,0:T(8,128)S(1)} %copy.42, bf16[2,2,4,10,128]{4,3,2,1,0:T(8,128)(2,1)S(1)} %get-tuple-element.29, bf16[2,2,4,10,128]{4,3,2,1,0:T(8,128)(2,1)S(1)} %get-tuple-element.28), kind=kOutput, calls=%fused_computation | convolution fusion | flops 441667584 | bytes 9234432 | tf_op jit(solution)/shard_map/rflqj,rkj->rflqk/dot_general | solution.py:317
  71.8 2.3 %fusion.18 = f32[2,2,4,5248]{3,2,1,0:T(4,128)S(1)} fusion(f32[2,2,4,10,5248]{4,3,2,1,0:T(8,128)S(1)} %convolution_multiply_fusion, bf16[2,5248,128]{2,1,0:T(8,128)(2,1)S(1)} %copy-done.1, bf16[2,5248,128]{2,1,0:T(8,128)(2,1)S(1)} %bitcast.66, f32[2,10,5248]{2,1,0:T(8,128)S(1)} %copy-done.2, bf16[2,2,4,10,128]{4,3,2,1,0:T(8,128)(2,1)S(1)} %get-tuple-element.29, ...), kind=kOutput, calls=%fused_computation.30 | convolution fusion | flops 443262976 | bytes 9570304 | tf_op jit(solution)/shard_map/rflqj,rkj->rflqk/dot_general | solution.py:316
  74.2 0.9 broadcast_multiply_fusion
  75.1 1.1 %fusion.3 = f32[2,2,4,10,256]{4,3,2,1,0:T(8,128)S(1)} fusion(bf16[2,5248,128]{2,1,0:T(8,128)(2,1)S(1)} %bitcast.67, bf16[2,5248,128]{2,1,0:T(8,128)(2,1)S(1)} %bitcast.64, f32[2,2,4,5248]{3,2,1,0:T(4,128)S(1)} %get-tuple-element.16, f32[2,10,5248]{2,1,0:T(8,128)S(1)} %copy.42), kind=kOutput, calls=%fused_computation.13 | convolution fusion | flops 443183104 | bytes 6293504 | tf_op jit(solution)/shard_map/rflqk,rkj->rflqj/dot_general | solution.py:333
  76.2 1.2 %fusion.20 = bf16[2,2,4,10,256]{4,3,2,1,0:T(8,128)(2,1)S(1)} fusion(f32[2,2,4,10,256]{4,3,2,1,0:T(8,128)S(1)} %fusion.3, bf16[2,5248,128]{2,1,0:T(8,128)(2,1)S(1)} %copy-done.1, bf16[2,5248,128]{2,1,0:T(8,128)(2,1)S(1)} %bitcast.68, f32[2,2,4,5248]{3,2,1,0:T(4,128)S(1)} %get-tuple-element.16, f32[2,10,5248]{2,1,0:T(8,128)S(1)} %copy-done.2), kind=kOutput, calls=%fused_computation.33 | convolution fusion | flops 442425344 | bytes 6375424 | tf_op jit(solution)/shard_map/rflqk,rkj->rflqj/dot_general | solution.py:331
  77.5 1.2 %fusion.16 = bf16[32,1280]{1,0:T(8,128)(2,1)S(1)} fusion(bf16[1280]{0:T(1024)(128)(2,1)S(1)} %fusion.46, s32[1280]{0:T(1024)S(1)} %copy-done.4, bf16[4,8,10,128]{3,2,1,0:T(8,128)(2,1)S(1)} %bitcast.76), kind=kOutput, calls=%fused_computation.26 | convolution fusion | flops 108175360 | bytes 171520 | tf_op jit(solution)/shard_map/dot_general | solution.py:336
  79.0 12.8 %all_to_all.10 = bf16[16,8,320]{2,1,0:T(8,128)(2,1)S(1)} all-to-all(bf16[16,8,320]{2,1,0:T(8,128)(2,1)S(1)} %reshape.481), channel_id=1, replica_groups=mesh['member'=2,'band'=4,'lev'=4] {'band','lev'}, dimensions={0} | all-to-all | bytes 163840 | tf_op jit(solution)/shard_map/all_to_all | solution.py:341
  91.9 0.2 fusion.17
  92.1 0.2 copy.45
  92.4 0.9 reshape.483.refs_2_
  93.3 9.3 %adjoint.1 = bf16[2,2,160,1281]{3,2,1,0:T(8,128)(2,1)} custom-call(s32[160,1]{1,0:T(8,128)} %copy.37.refs_6_.refs_0_, f32[16,256]{1,0:T(8,128)} %fusion.33.refs_7_.refs_1_, f32[10,8,256]{2,1,0:T(8,128)} %reshape.483.refs_2_, bf16[10,1296,256]{2,1,0:T(8,128)(2,1)} %get-tuple-element.5.refs_3_), custom_call_target="tpu_custom_call" | custom-call | tf_op jit(solution)/shard_map/adjoint/pallas_call | solution.py:221
  (79 shorter events, 3.4 us)
Async XLA Ops:
  0.6 41.0 %copy-start.5 = (s32[640]{0:T(1024)S(1)}, s32[640]{0:T(1024)}, u32[]{:S(2)}) copy-start(s32[640]{0:T(1024)} %param.8) | copy-start | bytes 7684
  0.6 40.4 %copy-start.9 = (s32[16]{0:T(128)S(1)}, s32[16]{0:T(128)}, u32[]{:S(2)}) copy-start(s32[16]{0:T(128)} %param.7) | copy-start | bytes 196
  0.7 31.6 %copy-start.8 = (s32[16]{0:T(128)S(1)}, s32[16]{0:T(128)}, u32[]{:S(2)}) copy-start(s32[16]{0:T(128)} %param.9) | copy-start | bytes 196
  32.6 8.7 %copy-start.6 = (s32[16]{0:T(128)}, s32[16]{0:T(128)S(1)}, u32[]{:S(2)}) copy-start(s32[16]{0:T(128)S(1)} %multiply_add_fusion.1) | copy-start | bytes 196
  33.7 24.9 %all-to-all-start = ((bf16[16,8,320]{2,1,0:T(8,128)(2,1)}), bf16[16,8,320]{2,1,0:T(8,128)(2,1)}, u32[]{:S(2)}, u32[]{:S(2)}) async-start(bf16[16,8,320]{2,1,0:T(8,128)(2,1)} %reshape.475), calls=%async_computation | async-start | bytes 196608 | tf_op jit(solution)/shard_map/all_to_all | solution.py:297
  45.9 5.0 %copy-start.3 = (bf16[2,4,5136]{2,1,0:T(4,128)(2,1)S(1)}, bf16[2,4,5136]{2,1,0:T(4,128)(2,1)}, u32[]{:S(2)}) copy-start(bf16[2,4,5136]{2,1,0:T(4,128)(2,1)} %param.6) | copy-start | bytes 246532
  68.2 3.6 %copy-start = (bf16[2,41,128,128]{3,2,1,0:T(8,128)(2,1)S(1)}, bf16[2,41,128,128]{3,2,1,0:T(8,128)(2,1)}, u32[]{:S(2)}) copy-start(bf16[2,41,128,128]{3,2,1,0:T(8,128)(2,1)} %get-tuple-element.25) | copy-start | bytes 8060932
  68.3 3.6 %copy-start.1 = (bf16[2,5248,128]{2,1,0:T(8,128)(2,1)S(1)}, bf16[2,5248,128]{2,1,0:T(8,128)(2,1)}, u32[]{:S(2)}) copy-start(bf16[2,5248,128]{2,1,0:T(8,128)(2,1)} %bitcast_negate_fusion) | copy-start | bytes 8060932
  68.3 3.6 %copy-start.2 = (f32[2,10,5248]{2,1,0:T(8,128)S(1)}, f32[2,10,5248]{2,1,0:T(8,128)}, u32[]{:S(2)}) copy-start(f32[2,10,5248]{2,1,0:T(8,128)} %copy.36) | copy-start | bytes 1259524
  76.2 1.3 %copy-start.4 = (s32[1280]{0:T(1024)S(1)}, s32[1280]{0:T(1024)}, u32[]{:S(2)}) copy-start(s32[1280]{0:T(1024)} %subtract_select_fusion) | copy-start | bytes 15364
  77.4 14.5 %copy-start.7 = (s32[16]{0:T(128)S(1)}, s32[16]{0:T(128)}, u32[]{:S(2)}) copy-start(s32[16]{0:T(128)} %copy-done.6) | copy-start | bytes 196

commit v3 on v2

--- a/solution.py
+++ b/solution.py
@@ -201,7 +201,7 @@
             tall, tall, tall, state, state,
             pltpu.VMEM((clusters, chunks * CHUNK, wide), jnp.bfloat16),
         ],
-        compiler_params=pltpu.CompilerParams(vmem_limit_bytes=58 * 2**20),
+        compiler_params=pltpu.CompilerParams(vmem_limit_bytes=26 * 2**20),
         name="legendre",
     )(
         ids, spread, lay(cos_lat[None, :]), lay(diag1), lay(diag2), lay(limit), limit,
@@ -229,7 +229,7 @@
         ],
         out_specs=pl.BlockSpec((2, 2, cluster, columns), lambda i: (0, 0, i, 0)),
         out_shape=jax.ShapeDtypeStruct((2, 2, pairs, columns), jnp.bfloat16),
-        compiler_params=pltpu.CompilerParams(vmem_limit_bytes=58 * 2**20),
+        compiler_params=pltpu.CompilerParams(vmem_limit_bytes=10 * 2**20),
         name="adjoint",
     )(limit, own_mask(cluster, rows), back, table)
 
@@ -250,23 +250,131 @@
     return jnp.cos(angles), jnp.sin(angles)
 
 
-def fourier_tables(lengths, high_count, blocks):
+TILES = 7
+
+
+def fourier_kernel(
+    blocks, length, stacked, weight, low_c, low_s, row_c, row_s, col_c, col_s, twl_c, twl_s,
+    twh_c, twh_s, grid, back, total,
+):
+    count = length[pl.program_id(0)]
+    fields = weight.shape[1]
+    half = fields // 2
+    chunks = row_c.shape[1]
+    total[...] = jnp.zeros_like(total)
+
+    @pl.loop(0, chunks)
+    def _(it):
+        base_c, base_s = low_c[0], low_s[0]
+        synth, analysis = [], []
+        for j in range(TILES):
+            far_c, far_s = col_c[0, it, :, j : j + 1], col_s[0, it, :, j : j + 1]
+            cosine = (base_c * far_c - base_s * far_s).astype(jnp.bfloat16)
+            sine = (base_s * far_c + base_c * far_s).astype(jnp.bfloat16)
+            synth.append((cosine, sine))
+            far_c, far_s = row_c[0, it, j : j + 1, :], row_s[0, it, j : j + 1, :]
+            cosine = (base_c * far_c - base_s * far_s).astype(jnp.bfloat16)
+            sine = (base_s * far_c + base_c * far_s).astype(jnp.bfloat16)
+            analysis.append((cosine, sine))
+        source = stacked[0]
+        added = total[...]
+        for j in range(TILES):
+            cosine, sine = synth[j]
+            table = jnp.concatenate(
+                [
+                    jnp.concatenate([cosine, sine], axis=1),
+                    jnp.concatenate([-sine, cosine], axis=1),
+                ],
+                axis=0,
+            )
+            both = jnp.dot(source, table, preferred_element_type=jnp.float32)
+            far_c, far_s = twh_c[0, it, :, j : j + 1], twh_s[0, it, :, j : j + 1]
+            near_c, near_s = twl_c[0], twl_s[0]
+            turn_c = near_c * far_c - near_s * far_s
+            turn_s = near_s * far_c + near_c * far_s
+            values = jnp.zeros((fields, LANES), jnp.float32)
+            for q in range(blocks):
+                rows = slice(q * fields, (q + 1) * fields)
+                values += turn_c[q : q + 1] * both[rows, :LANES]
+                values -= turn_s[q : q + 1] * both[rows, LANES:]
+            first = (it * TILES + j) * LANES
+            point = lax.broadcasted_iota(jnp.int32, (fields, LANES), 1) + first
+            values = jnp.where(point < count, values, 0.0)
+            lanes = pl.ds(pl.multiple_of(first, LANES), LANES)
+            grid[0, 0, :, lanes] = values[:half]
+            grid[0, 1, :, lanes] = values[half:]
+            weighted = values * weight[0, :, lanes]
+            turned = [
+                jnp.concatenate(
+                    [weighted * turn_c[q : q + 1], -(weighted * turn_s[q : q + 1])], axis=1
+                )
+                for q in range(blocks)
+            ]
+            turned = jnp.concatenate(turned, axis=0).astype(jnp.bfloat16)
+            cosine, sine = analysis[j]
+            table = jnp.concatenate(
+                [
+                    jnp.concatenate([cosine, -sine], axis=1),
+                    jnp.concatenate([sine, cosine], axis=1),
+                ],
+                axis=0,
+            )
+            added += jnp.dot(turned, table, preferred_element_type=jnp.float32)
+        total[...] = added
+
+    back[0] = total[...].astype(jnp.bfloat16)
+
+
+def fourier_both_ways(stacked, weight, lengths, blocks):
+    slots, rows, _ = stacked.shape
+    fields = rows // blocks
+    row_points = weight.shape[2]
+    chunks = -(-row_points // (TILES * LANES))
+    points = chunks * TILES * LANES
     low = jnp.arange(LANES, dtype=jnp.int32)
-    high = jnp.arange(high_count, dtype=jnp.int32) * LANES
+    high = jnp.arange(chunks * TILES, dtype=jnp.int32) * LANES
     inner = jnp.arange(SUBW, dtype=jnp.int32)
     outer = jnp.arange(blocks, dtype=jnp.int32) * SUBW
-    slots = lengths.shape[0]
-    low_c, low_s = (x[:, None] for x in angle_tables(lengths, inner, low))
-    high_c, high_s = (x[:, :, None] for x in angle_tables(lengths, inner, high))
-    shape = (slots, high_count * LANES, SUBW)
-    cosine = (low_c * high_c - low_s * high_s).astype(jnp.bfloat16).reshape(shape)
-    sine = (low_s * high_c + low_c * high_s).astype(jnp.bfloat16).reshape(shape)
-    low_c, low_s = (x[:, :, None] for x in angle_tables(lengths, low, outer))
-    high_c, high_s = (x[:, :, :, None] for x in angle_tables(lengths, high, outer))
-    shape = (slots, blocks, high_count * LANES)
-    twist_cos = (low_c * high_c - low_s * high_s).reshape(shape)
-    twist_sin = (low_s * high_c + low_c * high_s).reshape(shape)
-    return cosine, sine, twist_cos, twist_sin
+
+    def cut(x, y):
+        return x.reshape(slots, chunks, TILES, y)
+
+    def turn(x, y):
+        return jnp.swapaxes(cut(x, y), 2, 3)
+
+    low_c, low_s = angle_tables(lengths, inner, low)
+    high_c, high_s = angle_tables(lengths, inner, high)
+    twl_c, twl_s = angle_tables(lengths, low, outer)
+    twh_c, twh_s = angle_tables(lengths, outer, high)
+    weight = jnp.tile(weight.astype(jnp.float32), (1, 2, 1))
+    weight = jnp.pad(weight, ((0, 0), (0, 0), (0, points - row_points)))
+    operands = [
+        stacked, weight, low_c, low_s, cut(high_c, SUBW), cut(high_s, SUBW),
+        turn(high_c, SUBW), turn(high_s, SUBW), twl_c, twl_s, turn(twh_c, blocks),
+        turn(twh_s, blocks),
+    ]
+
+    def slot_block(shape):
+        return pl.BlockSpec((1,) + shape[1:], lambda i: (i,) + (0,) * (len(shape) - 1))
+
+    grid_shape = (slots, 2, fields // 2, points)
+
+    def kernel(*refs):
+        fourier_kernel(blocks, *refs)
+
+    return pl.pallas_call(
+        kernel,
+        grid=(slots,),
+        in_specs=[pl.BlockSpec(memory_space=pltpu.SMEM)] + [slot_block(x.shape) for x in operands],
+        out_specs=(slot_block(grid_shape), slot_block(stacked.shape)),
+        out_shape=(
+            jax.ShapeDtypeStruct(grid_shape, jnp.float32),
+            jax.ShapeDtypeStruct(stacked.shape, jnp.bfloat16),
+        ),
+        scratch_shapes=[pltpu.VMEM((rows, 2 * SUBW), jnp.float32)],
+        compiler_params=pltpu.CompilerParams(vmem_limit_bytes=24 * 2**20),
+        name="fourier",
+    )(lengths, *operands)
 
 
 def body(spec_in, observation_weight, latitude_row_length, wave_map, row_map):
@@ -305,33 +413,14 @@
     permute = jnp.where(m_of_w[:, None] == order[None, :], gain[None, :], 0.0).astype(jnp.bfloat16)
     scaled = jnp.dot(arrived, permute, preferred_element_type=jnp.float32).astype(jnp.bfloat16)
     scaled = scaled.reshape(row_cap, 2, levels, 2, blocks, SUBW)
+    stacked = jnp.transpose(scaled, (0, 4, 1, 2, 3, 5)).reshape(row_cap, -1, 2 * SUBW)
 
     slot_length = jnp.sum(jnp.where(chosen, latitude_row_length[None, :], 0), axis=1)
     lengths = lax.dynamic_slice_in_dim(slot_length, owner_index * row_cap, row_cap)
-    high_count = -(-row_points // LANES)
-    cosine, sine, twist_cos, twist_sin = fourier_tables(lengths, high_count, blocks)
-    stacked = jnp.concatenate([scaled[:, :, :, 0], scaled[:, :, :, 1]], axis=4)
-    table_re = jnp.concatenate([cosine, -sine], axis=2)
-    table_im = jnp.concatenate([sine, cosine], axis=2)
-    half_re = jnp.einsum("rflqj,rkj->rflqk", stacked, table_re, preferred_element_type=jnp.float32)
-    half_im = jnp.einsum("rflqj,rkj->rflqk", stacked, table_im, preferred_element_type=jnp.float32)
-    spread_cos = twist_cos[:, None, None]
-    spread_sin = twist_sin[:, None, None]
-    grid = jnp.sum(spread_cos * half_re - spread_sin * half_im, axis=3)
-    inside = jnp.arange(high_count * LANES, dtype=jnp.int32)[None, :] < lengths[:, None]
-    grid = jnp.where(inside[:, None, None], grid, 0.0)
+    grid, back = fourier_both_ways(stacked, observation_weight, lengths, blocks)
     grid_incr = grid[..., :row_points]
-
-    weight = jnp.pad(
-        observation_weight.astype(jnp.float32), ((0, 0), (0, 0), (0, high_count * LANES - row_points))
-    )
-    weighted = (grid * weight[:, None])[:, :, :, None]
-    turned_re = (weighted * spread_cos).astype(jnp.bfloat16)
-    turned_im = (-(weighted * spread_sin)).astype(jnp.bfloat16)
-    result = jnp.einsum(
-        "rflqk,rkj->rflqj", turned_re, table_re, preferred_element_type=jnp.float32
-    ) + jnp.einsum("rflqk,rkj->rflqj", turned_im, table_im, preferred_element_type=jnp.float32)
-    back = jnp.stack([result[..., :SUBW], result[..., SUBW:]], axis=3).astype(jnp.bfloat16)
+    back = back.reshape(row_cap, blocks, 2, levels, 2, SUBW)
+    back = jnp.transpose(back, (0, 2, 3, 4, 1, 5))
     back = back.reshape(-1, waves_all)
     back = lax.dot_general(
         back, permute, (((1,), (1,)), ((), ())), preferred_element_type=jnp.float32

time: 104 us -> 81.6 us (0.78)
  blocking collectives: 12.8 us -> 0 us
  matrix products: 12.2 us -> 2.49 us
  local copies, waits for them, and re-layouts: 22.1 us -> 12.5 us
  waiting for transfers between devices: 0.01 us -> 6.26 us
  starting transfers between devices: 7.34 us -> 13.3 us
  other arithmetic: 16.8 us -> 12.1 us
  Pallas kernels: 30.4 us -> 33.5 us
    all_to_all x1 -> x0, blocking collectives: 12.8 us -> none  [body(): lax.all_to_all(returning, ('band', 'lev'), split_axis=0, concat_axis=0, t...]
    pallas_call x0 -> x1, Pallas kernels: none -> 9.17 us  [fourier_both_ways(): pl.pallas_call(kernel, grid=(slots,), in_specs=[pl.BlockSpec(memory_space...]
    dot_general x4 -> x0, matrix products: 8.16 us -> none  [the longest x1 3.53 us: body(): jnp.einsum('rflqj,rkj->rflqk', stacked, table_im, preferred_element_type=...]
    sin x0 -> x5, other arithmetic: none -> 7.21 us  [angle_tables(): return (jnp.cos(angles), jnp.sin(angles))]
    all_to_all x0 -> x1, waiting for transfers between devices: none -> 6.26 us  [body(): lax.all_to_all(returning, ('band', 'lev'), split_axis=0, concat_axis=0, t...]
    all_to_all x0 -> x1, starting transfers between devices: none -> 6 us  [body(): lax.all_to_all(returning, ('band', 'lev'), split_axis=0, concat_axis=0, t...]
    unnamed x20 -> x14, local copies, waits for them, and re-layouts: 0.05 us -> 5.64 us
    sub x2 -> x0, local copies, waits for them, and re-layouts: 3.93 us -> none  [fourier_tables(): twist_cos = (low_c * high_c - low_s * high_s).reshape(shape)]
  transfers between devices with their start and end apart: 1 -> 2, of which waited for: 0 -> 1; matrix products, arithmetic and copies ran while one was open for 17% -> 14% of each run, Pallas kernels for 0% -> 0%
where the time goes in v3:
time: 81.6 us; the launch traced here: 81.3 us
  Pallas kernels  33.5 us (41%)
  starting transfers between devices  13.3 us (16%)
  local copies, waits for them, and re-layouts  12.5 us (15%)
  other arithmetic  12.1 us (15%)
  waiting for transfers between devices  6.26 us (8%)
  matrix products  2.49 us (3%)
  between operations  1.15 us (1%)
    pallas_call x1, Pallas kernels, legendre(): pl.pallas_call(kernel, grid=(chunks,), in_specs=[whole] * 9, out_specs=(p...  18.7 us
    pallas_call x1, Pallas kernels, fourier_both_ways(): pl.pallas_call(kernel, grid=(slots,), in_specs=[pl.BlockSpec(memory_space...  9.17 us
    all_to_all x1, starting transfers between devices, body(): lax.all_to_all(outgoing, ('band', 'lev'), split_axis=0, concat_axis=0, ti...  7.35 us
    sin x5, other arithmetic, angle_tables(): return (jnp.cos(angles), jnp.sin(angles))  7.21 us
    all_to_all x1, waiting for transfers between devices, body(): lax.all_to_all(returning, ('band', 'lev'), split_axis=0, concat_axis=0, t...  6.26 us
    all_to_all x1, starting transfers between devices, body(): lax.all_to_all(returning, ('band', 'lev'), split_axis=0, concat_axis=0, t...  6 us
    pallas_call x1, Pallas kernels, adjoint(): pl.pallas_call(kernel, grid=(pairs // cluster,), in_specs=[pl.BlockSpec((...  5.66 us
    unnamed x14, local copies, waits for them, and re-layouts  5.64 us
  transfers between devices with their start and end apart: 2, of which 1 were waited for; matrix products, arithmetic and copies ran while one was open for 14% of the time, Pallas kernels for 0%

profile of v3, /device:TPU:0, one launch (start us, length us, event | category | flops | bytes accessed | tf_op | source)
XLA Modules:
  0.0 81.3 jit_solution(8000991052502040954)
XLA Ops:
  0.7 0.9 %broadcast_subtract_fusion = (s32[160]{0:T(256)S(1)}, s32[160]{0:T(256)S(1)}) fusion(s32[640]{0:T(1024)} %param.8, s32[]{:T(128)S(6)} %select_n.131), kind=kLoop, calls=%fused_computation.113 | loop fusion | flops 160 | bytes 1924 | tf_op jit(solution)/shard_map/sub | solution.py:186
  1.6 0.1 tile.19
  1.7 0.3 select_reduce_fusion
  2.2 0.1 add.183
  2.5 0.1 add.189
  2.7 0.1 mul.221
  2.8 0.1 mul.222
  2.9 0.1 mul.229
  3.0 0.1 mul.230
  3.1 0.7 sine_log_fusion
  4.0 0.1 tile.21
  4.2 0.1 copy.39.refs_6_.refs_0_
  4.4 0.1 broadcast_in_dim.121
  4.6 0.3 and_convert_fusion.refs_1_
  4.9 18.7 %legendre.1 = (bf16[10,1296,256]{2,1,0:T(8,128)(2,1)S(1)}, f32[10,8,256]{2,1,0:T(8,128)S(1)}) custom-call(s32[2,256]{1,0:T(2,128)S(1)} %pad.22.refs_0_, bf16[256,1280]{1,0:T(8,128)(2,1)S(1)} %and_convert_fusion.refs_1_, f32[24,128]{1,0:T(8,128)S(1)} %pad.23.refs_2_, f32[24,128]{1,0:T(8,128)S(1)} %pad.24.refs_3_, f32[24,128]{1,0:T(8,128)S(1)} %pad.25.refs_4_, ...), custom_call_target="tpu_custom_call" | custom-call | tf_op jit(solution)/shard_map/legendre/pallas_call | solution.py:191
  23.6 2.7 %copy-done = bf16[10,1296,256]{2,1,0:T(8,128)(2,1)} copy-done((bf16[10,1296,256]{2,1,0:T(8,128)(2,1)}, bf16[10,1296,256]{2,1,0:T(8,128)(2,1)S(1)}, u32[]{:S(2)}) %copy-start) | copy-done | bytes 6635544
  26.4 0.3 reshape.358
  26.6 0.3 copy.40
  27.0 0.2 select_reduce_fusion.3
  27.2 0.3 convolution_convert_fusion
  27.5 0.8 %reshape.360 = bf16[16,8,320]{2,1,0:T(8,128)(2,1)} reshape(bf16[32,1280]{1,0:T(8,128)(2,1)S(1)} %convolution_convert_fusion) | data formatting | bytes 163840 | tf_op jit(solution)/shard_map/reshape | solution.py:404
  28.4 7.3 %all-to-all-start = ((bf16[16,8,320]{2,1,0:T(8,128)(2,1)}), bf16[16,8,320]{2,1,0:T(8,128)(2,1)S(1)}, u32[]{:S(2)}, u32[]{:S(2)}) async-start(bf16[16,8,320]{2,1,0:T(8,128)(2,1)} %reshape.360), calls=%async_computation | async-start | bytes 196608 | tf_op jit(solution)/shard_map/all_to_all | solution.py:405
  35.7 0.1 select_reduce_fusion.2
  36.2 0.1 broadcast_in_dim.122
  36.3 0.2 reshape.363
  36.6 1.7 %fusion.28 = f32[2,6,128,7]{2,0,3,1:T(2,128)S(1)} fusion(s32[6,128,7]{1,2,0:T(8,128)S(1)} %iota_multiply_fusion.1, s32[2]{0:T(128)S(1)} %get-tuple-element.22), kind=kLoop, calls=%fused_computation.52 | loop fusion | flops 75264 | bytes 64520 | tf_op jit(solution)/shard_map/convert_element_type | solution.py:247
  38.4 0.3 copy.43
  38.7 1.4 %fusion.18 = (f32[2,6,10,7]{3,2,1,0:T(8,128)S(1)}, f32[2,6,10,7]{3,2,1,0:T(8,128)S(1)}) fusion(f32[2]{0:T(128)S(1)} %convert_divide_fusion, s32[2]{0:T(128)S(1)} %get-tuple-element.22, s32[6,10,7]{2,1,0:T(8,128)S(1)} %broadcast_multiply_fusion), kind=kLoop, calls=%fused_computation.39 | loop fusion | flops 6720 | bytes 8416 | tf_op jit(solution)/shard_map/sin | solution.py:250
  40.0 2.9 %multiply_sine_fusion = (f32[2,6,128,7]{3,2,1,0:T(8,128)S(1)}, f32[2,6,128,7]{3,2,1,0:T(8,128)S(1)}) fusion(f32[2,6,128,7]{3,2,1,0:T(8,128)S(1)} %copy.43, f32[2]{0:T(128)S(1)} %convert_divide_fusion), kind=kLoop, calls=%fused_computation.18 | loop fusion | flops 10752 | bytes 129032 | tf_op jit(solution)/shard_map/sin | solution.py:250
  43.0 0.8 fusion.25
  43.7 0.3 fusion.31
  44.1 1.8 %fusion.13 = (f32[2,128,128]{2,1,0:T(8,128)S(1)}, f32[2,128,128]{2,1,0:T(8,128)S(1)}) fusion(f32[2]{0:T(128)S(1)} %convert_divide_fusion, s32[2]{0:T(128)S(1)} %get-tuple-element.22, s32[128,128]{1,0:T(8,128)S(1)} %iota_multiply_fusion), kind=kLoop, calls=%fused_computation.30 | loop fusion | flops 262144 | bytes 327696 | tf_op jit(solution)/shard_map/sin | solution.py:250
  45.9 0.1 tile.23
  46.2 0.1 reshape.362
  46.4 0.8 %fusion.8 = bf16[32,1280]{1,0:T(8,128)(2,1)S(1)} fusion(bf16[32,1280]{1,0:T(8,128)(2,1)S(1)} %reshape.362, bf16[1280]{0:T(1024)(128)(2,1)S(1)} %fusion.43, s32[1280]{0:T(1024)S(1)} %subtract_select_fusion), kind=kOutput, calls=%fused_computation.10 | convolution fusion | flops 108175360 | bytes 171520 | tf_op jit(solution)/shard_map/dot_general | solution.py:414
  47.4 9.2 %fourier.1 = (f32[2,2,4,5376]{3,2,1,0:T(4,128)S(1)}, bf16[2,80,256]{2,1,0:T(8,128)(2,1)S(1)}) custom-call(s32[2]{0:T(128)S(1)} %get-tuple-element.23.refs_0_, bf16[2,80,256]{2,1,0:T(8,128)(2,1)S(1)} %reshape.365.refs_1_, f32[2,8,5376]{2,1,0:T(8,128)S(1)} %pad.27.refs_2_, f32[2,128,128]{2,1,0:T(8,128)S(1)} %get-tuple-element.31.refs_3_, ...), custom_call_target="tpu_custom_call" | custom-call | tf_op jit(solution)/shard_map/fourier/pallas_call | solution.py:365
  56.6 1.2 %fusion.9 = bf16[32,1280]{1,0:T(8,128)(2,1)S(1)} fusion(bf16[1280]{0:T(1024)(128)(2,1)S(1)} %fusion.43, s32[1280]{0:T(1024)S(1)} %subtract_select_fusion, bf16[4,8,10,128]{3,2,1,0:T(8,128)(2,1)S(1)} %bitcast.34), kind=kOutput, calls=%fused_computation.11 | convolution fusion | flops 108175360 | bytes 171520 | tf_op jit(solution)/shard_map/dot_general | solution.py:425
  57.8 0.2 reshape.368
  58.1 0.7 reshape.369
  58.8 6.0 %all-to-all-start.1 = ((bf16[16,8,320]{2,1,0:T(8,128)(2,1)}), bf16[16,8,320]{2,1,0:T(8,128)(2,1)S(1)}, u32[]{:S(2)}, u32[]{:S(2)}) async-start(bf16[16,8,320]{2,1,0:T(8,128)(2,1)} %reshape.369), calls=%async_computation.1 | async-start | bytes 196608 | tf_op jit(solution)/shard_map/all_to_all | solution.py:430
  64.8 0.8 slice.3
  65.5 6.3 %all-to-all-done.1 = bf16[16,8,320]{2,1,0:T(8,128)(2,1)S(1)} async-done(((bf16[16,8,320]{2,1,0:T(8,128)(2,1)}), bf16[16,8,320]{2,1,0:T(8,128)(2,1)S(1)}, u32[]{:S(2)}, u32[]{:S(2)}) %all-to-all-start.1) | async-done | bytes 81952 | tf_op jit(solution)/shard_map/all_to_all | solution.py:430
  71.8 0.1 reshape.370
  72.0 0.2 fusion.10
  72.2 0.2 copy.46
  72.5 0.3 reshape.371.refs_2_
  72.7 2.9 %copy-done.1 = bf16[10,1296,256]{2,1,0:T(8,128)(2,1)S(1)} copy-done((bf16[10,1296,256]{2,1,0:T(8,128)(2,1)S(1)}, bf16[10,1296,256]{2,1,0:T(8,128)(2,1)}, u32[]{:S(2)}) %copy-start.1) | copy-done | bytes 6635544
  75.6 5.7 %adjoint.1 = bf16[2,2,160,1281]{3,2,1,0:T(8,128)(2,1)} custom-call(s32[160,1]{1,0:T(8,128)S(1)} %copy.39.refs_6_.refs_0_, f32[16,256]{1,0:T(8,128)S(1)} %fusion.33.refs_7_.refs_1_, f32[10,8,256]{2,1,0:T(8,128)S(1)} %reshape.371.refs_2_, bf16[10,1296,256]{2,1,0:T(8,128)(2,1)S(1)} %copy-done.1), custom_call_target="tpu_custom_call" | custom-call | tf_op jit(solution)/shard_map/adjoint/pallas_call | solution.py:221
  (69 shorter events, 2.1 us)
Async XLA Ops:
  0.6 4.3 %copy-start.2 = (bf16[2,2,1,160,1281]{4,3,2,1,0:T(8,128)(2,1)S(1)}, bf16[2,2,1,160,1281]{4,3,2,1,0:T(8,128)(2,1)}, u32[]{:S(2)}) copy-start(bf16[2,2,1,160,1281]{4,3,2,1,0:T(8,128)(2,1)} %param.5) | copy-start | bytes 4919044
  0.6 26.3 %copy-start.5 = (s32[16]{0:T(128)S(1)}, s32[16]{0:T(128)}, u32[]{:S(2)}) copy-start(s32[16]{0:T(128)} %param.9) | copy-start | bytes 196
  2.1 33.6 %copy-start.6 = (s32[16]{0:T(128)S(1)}, s32[16]{0:T(128)}, u32[]{:S(2)}) copy-start(s32[16]{0:T(128)} %param.7) | copy-start | bytes 196
  2.4 33.8 %copy-start.4 = (s32[640]{0:T(1024)S(1)}, s32[640]{0:T(1024)}, u32[]{:S(2)}) copy-start(s32[640]{0:T(1024)} %param.8) | copy-start | bytes 7684
  23.6 2.7 %copy-start = (bf16[10,1296,256]{2,1,0:T(8,128)(2,1)}, bf16[10,1296,256]{2,1,0:T(8,128)(2,1)S(1)}, u32[]{:S(2)}) copy-start(bf16[10,1296,256]{2,1,0:T(8,128)(2,1)S(1)} %get-tuple-element.9.refs_3_) | copy-start | bytes 19906564
  26.6 19.3 %copy-start.3 = (bf16[2,4,5136]{2,1,0:T(4,128)(2,1)S(1)}, bf16[2,4,5136]{2,1,0:T(4,128)(2,1)}, u32[]{:S(2)}) copy-start(bf16[2,4,5136]{2,1,0:T(4,128)(2,1)} %param.6) | copy-start | bytes 246532
  28.4 17.7 %all-to-all-start = ((bf16[16,8,320]{2,1,0:T(8,128)(2,1)}), bf16[16,8,320]{2,1,0:T(8,128)(2,1)S(1)}, u32[]{:S(2)}, u32[]{:S(2)}) async-start(bf16[16,8,320]{2,1,0:T(8,128)(2,1)} %reshape.360), calls=%async_computation | async-start | bytes 196608 | tf_op jit(solution)/shard_map/all_to_all | solution.py:405
  58.8 13.0 %all-to-all-start.1 = ((bf16[16,8,320]{2,1,0:T(8,128)(2,1)}), bf16[16,8,320]{2,1,0:T(8,128)(2,1)S(1)}, u32[]{:S(2)}, u32[]{:S(2)}) async-start(bf16[16,8,320]{2,1,0:T(8,128)(2,1)} %reshape.369), calls=%async_computation.1 | async-start | bytes 196608 | tf_op jit(solution)/shard_map/all_to_all | solution.py:430
  72.7 2.9 %copy-start.1 = (bf16[10,1296,256]{2,1,0:T(8,128)(2,1)S(1)}, bf16[10,1296,256]{2,1,0:T(8,128)(2,1)}, u32[]{:S(2)}) copy-start(bf16[10,1296,256]{2,1,0:T(8,128)(2,1)} %copy-done) | copy-start | bytes 19906564

commit v4 on v3

--- a/solution.py
+++ b/solution.py
@@ -40,7 +40,7 @@
 
 def legendre_kernel(
     truncation, groups, group_pad, blocks, part, cluster, ids, spread, mu, diag1, diag2, bound,
-    limit, own, spec, out, fourier, slopes, laggeds, values, newer, older, kept,
+    limit, own, spec, out, fourier, slopes, laggeds, values, newer, older, kept, epsilon, sems,
 ):
     step = pl.program_id(0)
     half = groups // blocks
@@ -51,6 +51,7 @@
     def _():
         newer[...] = jnp.zeros_like(newer)
         older[...] = diag1[...]
+        epsilon[...] = jnp.zeros_like(epsilon)
 
     column = lax.broadcasted_iota(jnp.int32, (CHUNK, 256), 0) + step * CHUNK
     lane = lax.broadcasted_iota(jnp.int32, (CHUNK, 256), 1)
@@ -72,15 +73,15 @@
         restart_first = column == 0
         restart = restart_first | (column == boundary)
 
-        def squared(v):
-            upper = jnp.maximum(v * v - order_m * order_m, 0.0)
-            lower = jnp.maximum(4.0 * v * v - 1.0, 1.0)
-            return upper / lower
-
-        inverse = lax.rsqrt(jnp.where(restart, 1.0, squared(degree)))
+        upper = jnp.maximum(degree * degree - order_m * order_m, 0.0)
+        lower = jnp.maximum(4.0 * degree * degree - 1.0, 1.0)
+        ratio = upper / lower
+        inverse = lax.rsqrt(jnp.where(restart, 1.0, ratio))
         slope = jnp.where(restart, 0.0, inverse)
-        lagged = jnp.where(restart, 0.0, -jnp.sqrt(squared(degree - 1.0)) * inverse)
-        lagged = jnp.where(restart_first, 1.0, lagged)
+        epsilon[b, 8:, :] = ratio * inverse
+        before = epsilon[b, 7 : 7 + CHUNK, :]
+        epsilon[b, 0:8, :] = epsilon[b, CHUNK : CHUNK + 8, :]
+        lagged = jnp.where(restart_first, 1.0, -(before * slope))
         for table, compact in ((slopes, slope), (laggeds, lagged)):
             wide = jnp.dot(split(compact), spread[...], preferred_element_type=jnp.float32)
             for g in range(half):
@@ -107,8 +108,13 @@
     for g in range(groups):
         piece = values[pl.ds(g, CHUNK, stride=group_pad), :].astype(jnp.bfloat16)
         lanes = pl.ds((g % tiles) * LANES, LANES)
-        out[g // tiles, :, lanes] = piece
         kept[g // tiles, here, lanes] = piece
+
+    def outward(i):
+        rows = pl.ds(pl.multiple_of(i * CHUNK, CHUNK), CHUNK)
+        return pltpu.make_async_copy(kept.at[:, rows, :], out.at[:, rows, :], sems.at[i])
+
+    outward(step).start()
 
     @pl.when(step == pl.num_programs(0) - 1)
     def _():
@@ -129,6 +135,8 @@
             )
             product = product.reshape(8, cluster, wide_lanes) * own[...][None]
             fourier[k] = jnp.sum(product, axis=1)
+        for i in range(kept.shape[1] // CHUNK):
+            outward(i).wait()
 
 
 def adjoint_kernel(cluster, normaliser, limit, own, back, table, out):
@@ -192,7 +200,7 @@
         kernel,
         grid=(chunks,),
         in_specs=[whole] * 9,
-        out_specs=(pl.BlockSpec((clusters, CHUNK, wide), lambda i: (0, i, 0)), whole),
+        out_specs=(pl.BlockSpec(memory_space=pltpu.HBM), whole),
         out_shape=(
             jax.ShapeDtypeStruct((clusters, chunks * CHUNK, wide), jnp.bfloat16),
             jax.ShapeDtypeStruct((clusters, 8, wide), jnp.float32),
@@ -200,6 +208,8 @@
         scratch_shapes=[
             tall, tall, tall, state, state,
             pltpu.VMEM((clusters, chunks * CHUNK, wide), jnp.bfloat16),
+            pltpu.VMEM((blocks, CHUNK + 8, 256), jnp.float32),
+            pltpu.SemaphoreType.DMA((chunks,)),
         ],
         compiler_params=pltpu.CompilerParams(vmem_limit_bytes=26 * 2**20),
         name="legendre",
@@ -241,38 +251,36 @@
     return slot_of_row[None, :] == jnp.arange(owners * row_cap, dtype=jnp.int32)[:, None]
 
 
-def angle_tables(lengths, orders, points):
-    safe_len = jnp.maximum(lengths, 1)[:, None, None]
-    step_angle = 2.0 * math.pi / safe_len.astype(jnp.float32)
-    angles = (points[None, :, None] * orders[None, None, :] % safe_len).astype(
-        jnp.float32
-    ) * step_angle
-    return jnp.cos(angles), jnp.sin(angles)
-
-
 TILES = 7
 
 
 def fourier_kernel(
-    blocks, length, stacked, weight, low_c, low_s, row_c, row_s, col_c, col_s, twl_c, twl_s,
-    twh_c, twh_s, grid, back, total,
+    blocks, length, stacked, weight, trig_c, trig_s, col_c, col_s, twh_c, twh_s, grid, back,
+    total, low_c, low_s,
 ):
     count = length[pl.program_id(0)]
     fields = weight.shape[1]
     half = fields // 2
-    chunks = row_c.shape[1]
+    chunks = col_c.shape[1]
     total[...] = jnp.zeros_like(total)
+    unit_c, unit_s = trig_c[0, 0:8, :], trig_s[0, 0:8, :]
+    for a in range(LANES // 8):
+        far_c, far_s = trig_c[0, 8 + a : 9 + a, :], trig_s[0, 8 + a : 9 + a, :]
+        low_c[8 * a : 8 * a + 8, :] = unit_c * far_c - unit_s * far_s
+        low_s[8 * a : 8 * a + 8, :] = unit_s * far_c + unit_c * far_s
+    turn_row = trig_c.shape[1] - 16
 
     @pl.loop(0, chunks)
     def _(it):
-        base_c, base_s = low_c[0], low_s[0]
+        base_c, base_s = low_c[...], low_s[...]
         synth, analysis = [], []
         for j in range(TILES):
             far_c, far_s = col_c[0, it, :, j : j + 1], col_s[0, it, :, j : j + 1]
             cosine = (base_c * far_c - base_s * far_s).astype(jnp.bfloat16)
             sine = (base_s * far_c + base_c * far_s).astype(jnp.bfloat16)
             synth.append((cosine, sine))
-            far_c, far_s = row_c[0, it, j : j + 1, :], row_s[0, it, j : j + 1, :]
+            row = pl.ds(24 + it * TILES + j, 1)
+            far_c, far_s = trig_c[0, row, :], trig_s[0, row, :]
             cosine = (base_c * far_c - base_s * far_s).astype(jnp.bfloat16)
             sine = (base_s * far_c + base_c * far_s).astype(jnp.bfloat16)
             analysis.append((cosine, sine))
@@ -289,7 +297,8 @@
             )
             both = jnp.dot(source, table, preferred_element_type=jnp.float32)
             far_c, far_s = twh_c[0, it, :, j : j + 1], twh_s[0, it, :, j : j + 1]
-            near_c, near_s = twl_c[0], twl_s[0]
+            rows = slice(turn_row, turn_row + blocks)
+            near_c, near_s = trig_c[0, rows, :], trig_s[0, rows, :]
             turn_c = near_c * far_c - near_s * far_s
             turn_s = near_s * far_c + near_c * far_s
             values = jnp.zeros((fields, LANES), jnp.float32)
@@ -331,27 +340,31 @@
     row_points = weight.shape[2]
     chunks = -(-row_points // (TILES * LANES))
     points = chunks * TILES * LANES
-    low = jnp.arange(LANES, dtype=jnp.int32)
-    high = jnp.arange(chunks * TILES, dtype=jnp.int32) * LANES
-    inner = jnp.arange(SUBW, dtype=jnp.int32)
+    tiles = chunks * TILES
+    lane = jnp.arange(LANES, dtype=jnp.int32)
     outer = jnp.arange(blocks, dtype=jnp.int32) * SUBW
-
-    def cut(x, y):
-        return x.reshape(slots, chunks, TILES, y)
-
-    def turn(x, y):
-        return jnp.swapaxes(cut(x, y), 2, 3)
-
-    low_c, low_s = angle_tables(lengths, inner, low)
-    high_c, high_s = angle_tables(lengths, inner, high)
-    twl_c, twl_s = angle_tables(lengths, low, outer)
-    twh_c, twh_s = angle_tables(lengths, outer, high)
+    outer = jnp.pad(outer, (0, 16 - blocks))
+    high = jnp.pad(lane[:tiles] * LANES, (0, -tiles % 8))
+    factors = jnp.concatenate([lane[:8], lane[: LANES // 8] * 8, high, outer])
+    products = factors[:, None] * lane[None, :]
+    products = jnp.concatenate([products, outer[:, None] * (lane * LANES)[None, :]])
+    safe_len = jnp.maximum(lengths, 1)[:, None, None]
+    angles = (products[None] % safe_len).astype(jnp.float32)
+    angles = angles * (2.0 * math.pi / safe_len.astype(jnp.float32))
+    turn_row = 24 + high.shape[0]
+
+    def arrange(x):
+        col = x[:, 24 : 24 + tiles].reshape(slots, chunks, TILES, LANES)
+        far = x[:, turn_row + 16 : turn_row + 16 + blocks, :tiles]
+        far = far.reshape(slots, blocks, chunks, TILES)
+        return x[:, : turn_row + 16], jnp.swapaxes(col, 2, 3), jnp.swapaxes(far, 1, 2)
+
+    trig_c, col_c, twh_c = arrange(jnp.cos(angles))
+    trig_s, col_s, twh_s = arrange(jnp.sin(angles))
     weight = jnp.tile(weight.astype(jnp.float32), (1, 2, 1))
     weight = jnp.pad(weight, ((0, 0), (0, 0), (0, points - row_points)))
     operands = [
-        stacked, weight, low_c, low_s, cut(high_c, SUBW), cut(high_s, SUBW),
-        turn(high_c, SUBW), turn(high_s, SUBW), twl_c, twl_s, turn(twh_c, blocks),
-        turn(twh_s, blocks),
+        stacked, weight, trig_c, trig_s, col_c, col_s, twh_c, twh_s,
     ]
 
     def slot_block(shape):
@@ -371,7 +384,11 @@
             jax.ShapeDtypeStruct(grid_shape, jnp.float32),
             jax.ShapeDtypeStruct(stacked.shape, jnp.bfloat16),
         ),
-        scratch_shapes=[pltpu.VMEM((rows, 2 * SUBW), jnp.float32)],
+        scratch_shapes=[
+            pltpu.VMEM((rows, 2 * SUBW), jnp.float32),
+            pltpu.VMEM((LANES, SUBW), jnp.float32),
+            pltpu.VMEM((LANES, SUBW), jnp.float32),
+        ],
         compiler_params=pltpu.CompilerParams(vmem_limit_bytes=24 * 2**20),
         name="fourier",
     )(lengths, *operands)

time: 81.6 us -> 73.8 us (0.904)
  other arithmetic: 12.1 us -> 4.54 us
  waiting for transfers between devices: 6.26 us -> 9.34 us
  starting transfers between devices: 13.3 us -> 10.9 us
  Pallas kernels: 33.5 us -> 31.5 us
  local copies, waits for them, and re-layouts: 12.5 us -> 13.4 us
    sin x5 -> x1, other arithmetic: 7.21 us -> 1.5 us  [fourier_both_ways(): trig_s, col_s, twh_s = arrange(jnp.sin(angles))]
    all_to_all x1, waiting for transfers between devices: 0.01 us -> 3.12 us  [body(): lax.all_to_all(outgoing, ('band', 'lev'), split_axis=0, concat_axis=0, ti...]
    all_to_all x1, starting transfers between devices: 6 us -> 3.51 us  [body(): lax.all_to_all(returning, ('band', 'lev'), split_axis=0, concat_axis=0, t...]
    pallas_call x1, Pallas kernels: 18.7 us -> 16.8 us  [legendre(): pl.pallas_call(kernel, grid=(chunks,), in_specs=[whole] * 9, out_specs=(p...]
    convert_element_type x1 -> x0, other arithmetic: 1.74 us -> none  [angle_tables(): (points[None, :, None] * orders[None, None, :] % safe_len).astype(jnp.flo...]
    reshape x0 -> x4, local copies, waits for them, and re-layouts: none -> 0.91 us  [the longest x2 0.58 us: arrange(): col = x[:, 24:24 + tiles].reshape(slots, chunks, TILES, LANES)]
  transfers between devices with their start and end apart: 2 -> 2, of which waited for: 1 -> 2; matrix products, arithmetic and copies ran while one was open for 14% -> 6% of each run, Pallas kernels for 0% -> 0%
where the time goes in v4:
time: 73.8 us; the launch traced here: 73.4 us
  Pallas kernels  31.5 us (43%)
  local copies, waits for them, and re-layouts  13.4 us (18%)
  starting transfers between devices  10.9 us (15%)
  waiting for transfers between devices  9.34 us (13%)
  other arithmetic  4.54 us (6%)
  matrix products  2.49 us (3%)
  between operations  1.21 us (2%)
    pallas_call x1, Pallas kernels, legendre(): pl.pallas_call(kernel, grid=(chunks,), in_specs=[whole] * 9, out_specs=(p...  16.8 us
    pallas_call x1, Pallas kernels, fourier_both_ways(): pl.pallas_call(kernel, grid=(slots,), in_specs=[pl.BlockSpec(memory_space...  9.07 us
    all_to_all x1, starting transfers between devices, body(): lax.all_to_all(outgoing, ('band', 'lev'), split_axis=0, concat_axis=0, ti...  7.35 us
    all_to_all x1, waiting for transfers between devices, body(): lax.all_to_all(returning, ('band', 'lev'), split_axis=0, concat_axis=0, t...  6.21 us
    pallas_call x1, Pallas kernels, adjoint(): pl.pallas_call(kernel, grid=(pairs // cluster,), in_specs=[pl.BlockSpec((...  5.69 us
    unnamed x14, local copies, waits for them, and re-layouts  5.65 us
    all_to_all x1, starting transfers between devices, body(): lax.all_to_all(returning, ('band', 'lev'), split_axis=0, concat_axis=0, t...  3.51 us
    all_to_all x1, waiting for transfers between devices, body(): lax.all_to_all(outgoing, ('band', 'lev'), split_axis=0, concat_axis=0, ti...  3.12 us
  transfers between devices with their start and end apart: 2, of which 2 were waited for; matrix products, arithmetic and copies ran while one was open for 6% of the time, Pallas kernels for 0%

profile of v4, /device:TPU:0, one launch (start us, length us, event | category | flops | bytes accessed | tf_op | source)
XLA Modules:
  0.0 73.4 jit_solution(9609482703318926047)
XLA Ops:
  0.7 0.9 %broadcast_subtract_fusion = (s32[160]{0:T(256)S(1)}, s32[160]{0:T(256)S(1)}) fusion(s32[640]{0:T(1024)} %param.8, s32[]{:T(128)S(6)} %select_n.103), kind=kLoop, calls=%fused_computation.84 | loop fusion | flops 160 | bytes 1924 | tf_op jit(solution)/shard_map/sub | solution.py:194
  1.7 0.3 select_reduce_fusion
  2.2 0.1 add.146
  2.4 0.1 add.151
  2.5 0.1 add.152
  2.7 0.1 mul.125
  2.8 0.1 mul.126
  2.9 0.1 mul.133
  3.0 0.1 mul.134
  3.1 0.7 sine_log_fusion
  4.2 0.1 copy.45.refs_6_.refs_0_
  4.4 0.1 broadcast_in_dim.115
  4.7 0.3 and_convert_fusion.refs_1_
  4.9 16.8 %legendre.1 = (bf16[10,1296,256]{2,1,0:T(8,128)(2,1)S(1)}, f32[10,8,256]{2,1,0:T(8,128)S(1)}) custom-call(s32[2,256]{1,0:T(2,128)S(1)} %pad.30.refs_0_, bf16[256,1280]{1,0:T(8,128)(2,1)S(1)} %and_convert_fusion.refs_1_, f32[24,128]{1,0:T(8,128)S(1)} %pad.31.refs_2_, f32[24,128]{1,0:T(8,128)S(1)} %pad.32.refs_3_, f32[24,128]{1,0:T(8,128)S(1)} %pad.33.refs_4_, ...), custom_call_target="tpu_custom_call" | custom-call | tf_op jit(solution)/shard_map/legendre/pallas_call | solution.py:199
  21.7 2.7 %copy-done = bf16[10,1296,256]{2,1,0:T(8,128)(2,1)} copy-done((bf16[10,1296,256]{2,1,0:T(8,128)(2,1)}, bf16[10,1296,256]{2,1,0:T(8,128)(2,1)S(1)}, u32[]{:S(2)}) %copy-start) | copy-done | bytes 6635544
  24.5 0.3 reshape.257
  24.7 0.3 copy.46
  25.1 0.2 select_reduce_fusion.3
  25.3 0.3 convolution_convert_fusion
  25.6 0.8 %reshape.259 = bf16[16,8,320]{2,1,0:T(8,128)(2,1)} reshape(bf16[32,1280]{1,0:T(8,128)(2,1)S(1)} %convolution_convert_fusion) | data formatting | bytes 163840 | tf_op jit(solution)/shard_map/reshape | solution.py:421
  26.5 7.4 %all-to-all-start = ((bf16[16,8,320]{2,1,0:T(8,128)(2,1)}), bf16[16,8,320]{2,1,0:T(8,128)(2,1)S(1)}, u32[]{:S(2)}, u32[]{:S(2)}) async-start(bf16[16,8,320]{2,1,0:T(8,128)(2,1)} %reshape.259), calls=%async_computation | async-start | bytes 196608 | tf_op jit(solution)/shard_map/all_to_all | solution.py:422
  33.8 0.1 select_reduce_fusion.2
  34.0 0.1 broadcast_in_dim.116
  34.1 0.2 reshape.262
  34.7 1.5 %fusion.13 = (f32[2,104,128]{2,1,0:T(8,128)S(1)}, f32[2,104,128]{2,1,0:T(8,128)S(1)}) fusion(f32[2]{0:T(128)S(1)} %convert_divide_fusion, s32[2]{0:T(128)S(1)} %get-tuple-element.20, s32[104,128]{1,0:T(8,128)S(1)} %pad_add_fusion), kind=kLoop, calls=%fused_computation.24 | loop fusion | flops 212992 | bytes 266256 | tf_op jit(solution)/shard_map/sin | solution.py:363
  36.3 0.3 copy.50
  36.7 0.3 copy.52
  37.0 0.1 copy.53
  37.1 0.2 copy.54
  37.2 0.1 copy.55
  37.3 0.2 copy.56
  37.6 0.1 tile.23
  37.7 3.1 %all-to-all-done = bf16[16,8,320]{2,1,0:T(8,128)(2,1)S(1)} async-done(((bf16[16,8,320]{2,1,0:T(8,128)(2,1)}), bf16[16,8,320]{2,1,0:T(8,128)(2,1)S(1)}, u32[]{:S(2)}, u32[]{:S(2)}) %all-to-all-start) | async-done | bytes 81952 | tf_op jit(solution)/shard_map/all_to_all | solution.py:422
  41.0 0.1 reshape.261
  41.1 0.8 %fusion.8 = bf16[32,1280]{1,0:T(8,128)(2,1)S(1)} fusion(bf16[32,1280]{1,0:T(8,128)(2,1)S(1)} %reshape.261, bf16[1280]{0:T(1024)(128)(2,1)S(1)} %fusion.27, s32[1280]{0:T(1024)S(1)} %subtract_select_fusion), kind=kOutput, calls=%fused_computation.10 | convolution fusion | flops 108175360 | bytes 171520 | tf_op jit(solution)/shard_map/dot_general | solution.py:431
  42.1 9.1 %fourier.1 = (f32[2,2,4,5376]{3,2,1,0:T(4,128)S(1)}, bf16[2,80,256]{2,1,0:T(8,128)(2,1)S(1)}) custom-call(s32[2]{0:T(128)S(1)} %get-tuple-element.21.refs_0_, bf16[2,80,256]{2,1,0:T(8,128)(2,1)S(1)} %reshape.264.refs_1_, f32[2,8,5376]{2,1,0:T(8,128)S(1)} %pad.35.refs_2_, f32[2,88,128]{2,1,0:T(8,128)S(1)} %slice.40.refs_3_, f32[2,88,128]{2,1,0:T(8,128)S(1)} %slice.41.refs_4_, ...), custom_call_target="tpu_custom_call" | custom-call | tf_op jit(solution)/shard_map/fourier/pallas_call | solution.py:378
  51.3 1.2 %fusion.9 = bf16[32,1280]{1,0:T(8,128)(2,1)S(1)} fusion(bf16[1280]{0:T(1024)(128)(2,1)S(1)} %fusion.27, s32[1280]{0:T(1024)S(1)} %subtract_select_fusion, bf16[4,8,10,128]{3,2,1,0:T(8,128)(2,1)S(1)} %bitcast.51), kind=kOutput, calls=%fused_computation.11 | convolution fusion | flops 108175360 | bytes 171520 | tf_op jit(solution)/shard_map/dot_general | solution.py:442
  52.4 0.2 reshape.271
  52.7 0.7 reshape.272
  53.4 3.5 %all-to-all-start.1 = ((bf16[16,8,320]{2,1,0:T(8,128)(2,1)}), bf16[16,8,320]{2,1,0:T(8,128)(2,1)S(1)}, u32[]{:S(2)}, u32[]{:S(2)}) async-start(bf16[16,8,320]{2,1,0:T(8,128)(2,1)} %reshape.272), calls=%async_computation.1 | async-start | bytes 196608 | tf_op jit(solution)/shard_map/all_to_all | solution.py:447
  56.9 0.8 %slice.39 = f32[2,2,4,5136]{3,2,1,0:T(4,128)} slice(f32[2,2,4,5376]{3,2,1,0:T(4,128)S(1)} %get-tuple-element.7), slice={[0:2], [0:2], [0:4], [0:5136]} | slice | bytes 657408 | tf_op jit(solution)/shard_map/slice | solution.py:438
  57.7 6.2 %all-to-all-done.1 = bf16[16,8,320]{2,1,0:T(8,128)(2,1)S(1)} async-done(((bf16[16,8,320]{2,1,0:T(8,128)(2,1)}), bf16[16,8,320]{2,1,0:T(8,128)(2,1)S(1)}, u32[]{:S(2)}, u32[]{:S(2)}) %all-to-all-start.1) | async-done | bytes 81952 | tf_op jit(solution)/shard_map/all_to_all | solution.py:447
  63.9 0.1 reshape.273
  64.0 0.2 fusion.10
  64.2 0.2 copy.59
  64.5 0.3 reshape.274.refs_2_
  64.8 2.9 %copy-done.1 = bf16[10,1296,256]{2,1,0:T(8,128)(2,1)S(1)} copy-done((bf16[10,1296,256]{2,1,0:T(8,128)(2,1)S(1)}, bf16[10,1296,256]{2,1,0:T(8,128)(2,1)}, u32[]{:S(2)}) %copy-start.1) | copy-done | bytes 6635544
  67.7 5.7 %adjoint.1 = bf16[2,2,160,1281]{3,2,1,0:T(8,128)(2,1)} custom-call(s32[160,1]{1,0:T(8,128)S(1)} %copy.45.refs_6_.refs_0_, f32[16,256]{1,0:T(8,128)S(1)} %fusion.18.refs_7_.refs_1_, f32[10,8,256]{2,1,0:T(8,128)S(1)} %reshape.274.refs_2_, bf16[10,1296,256]{2,1,0:T(8,128)(2,1)S(1)} %copy-done.1), custom_call_target="tpu_custom_call" | custom-call | tf_op jit(solution)/shard_map/adjoint/pallas_call | solution.py:231
  (82 shorter events, 2.2 us)
Async XLA Ops:
  0.6 4.3 %copy-start.2 = (bf16[2,2,1,160,1281]{4,3,2,1,0:T(8,128)(2,1)S(1)}, bf16[2,2,1,160,1281]{4,3,2,1,0:T(8,128)(2,1)}, u32[]{:S(2)}) copy-start(bf16[2,2,1,160,1281]{4,3,2,1,0:T(8,128)(2,1)} %param.5) | copy-start | bytes 4919044
  0.6 24.4 %copy-start.5 = (s32[16]{0:T(128)S(1)}, s32[16]{0:T(128)}, u32[]{:S(2)}) copy-start(s32[16]{0:T(128)} %param.9) | copy-start | bytes 196
  2.1 31.7 %copy-start.6 = (s32[16]{0:T(128)S(1)}, s32[16]{0:T(128)}, u32[]{:S(2)}) copy-start(s32[16]{0:T(128)} %param.7) | copy-start | bytes 196
  2.1 31.8 %copy-start.4 = (s32[640]{0:T(1024)S(1)}, s32[640]{0:T(1024)}, u32[]{:S(2)}) copy-start(s32[640]{0:T(1024)} %param.8) | copy-start | bytes 7684
  21.7 2.8 %copy-start = (bf16[10,1296,256]{2,1,0:T(8,128)(2,1)}, bf16[10,1296,256]{2,1,0:T(8,128)(2,1)S(1)}, u32[]{:S(2)}) copy-start(bf16[10,1296,256]{2,1,0:T(8,128)(2,1)S(1)} %get-tuple-element.9.refs_3_) | copy-start | bytes 19906564
  24.5 13.0 %copy-start.3 = (bf16[2,4,5136]{2,1,0:T(4,128)(2,1)S(1)}, bf16[2,4,5136]{2,1,0:T(4,128)(2,1)}, u32[]{:S(2)}) copy-start(bf16[2,4,5136]{2,1,0:T(4,128)(2,1)} %param.6) | copy-start | bytes 246532
  26.5 14.4 %all-to-all-start = ((bf16[16,8,320]{2,1,0:T(8,128)(2,1)}), bf16[16,8,320]{2,1,0:T(8,128)(2,1)S(1)}, u32[]{:S(2)}, u32[]{:S(2)}) async-start(bf16[16,8,320]{2,1,0:T(8,128)(2,1)} %reshape.259), calls=%async_computation | async-start | bytes 196608 | tf_op jit(solution)/shard_map/all_to_all | solution.py:422
  53.4 10.5 %all-to-all-start.1 = ((bf16[16,8,320]{2,1,0:T(8,128)(2,1)}), bf16[16,8,320]{2,1,0:T(8,128)(2,1)S(1)}, u32[]{:S(2)}, u32[]{:S(2)}) async-start(bf16[16,8,320]{2,1,0:T(8,128)(2,1)} %reshape.272), calls=%async_computation.1 | async-start | bytes 196608 | tf_op jit(solution)/shard_map/all_to_all | solution.py:447
  64.8 2.9 %copy-start.1 = (bf16[10,1296,256]{2,1,0:T(8,128)(2,1)S(1)}, bf16[10,1296,256]{2,1,0:T(8,128)(2,1)}, u32[]{:S(2)}) copy-start(bf16[10,1296,256]{2,1,0:T(8,128)(2,1)} %copy-done) | copy-start | bytes 19906564

commit v5 on v4

--- a/solution.py
+++ b/solution.py
@@ -211,7 +211,7 @@
             pltpu.VMEM((blocks, CHUNK + 8, 256), jnp.float32),
             pltpu.SemaphoreType.DMA((chunks,)),
         ],
-        compiler_params=pltpu.CompilerParams(vmem_limit_bytes=26 * 2**20),
+        compiler_params=pltpu.CompilerParams(vmem_limit_bytes=54 * 2**20),
         name="legendre",
     )(
         ids, spread, lay(cos_lat[None, :]), lay(diag1), lay(diag2), lay(limit), limit,

time: 73.8 us -> 78.8 us (1.068)
  other arithmetic: 4.54 us -> 6.77 us
  Pallas kernels: 31.5 us -> 33.5 us
  local copies, waits for them, and re-layouts: 13.4 us -> 14.3 us
    unnamed x14, local copies, waits for them, and re-layouts: 5.65 us -> 2.91 us
    pad x4, local copies, waits for them, and re-layouts: 0.03 us -> 2.42 us  [lay(): return jnp.pad(x, ((0, group_pad - groups), (0, 0)))]
    pallas_call x1, Pallas kernels: 16.8 us -> 18.7 us  [legendre(): pl.pallas_call(kernel, grid=(chunks,), in_specs=[whole] * 9, out_specs=(p...]
    convert_element_type x1, other arithmetic: 0.01 us -> 0.93 us  [body(): fourier.astype(jnp.bfloat16).reshape(clusters, 2, 2, 2, cluster, rows)]
    convert_element_type x1, other arithmetic: 0.26 us -> 1.1 us  [legendre(): ((source % part == target) & (source < 3 * part)).astype(jnp.bfloat16)]
where the time goes in v5:
time: 78.8 us; the launch traced here: 78.4 us
  Pallas kernels  33.5 us (43%)
  local copies, waits for them, and re-layouts  14.3 us (18%)
  starting transfers between devices  10.9 us (14%)
  waiting for transfers between devices  9.34 us (12%)
  other arithmetic  6.77 us (9%)
  matrix products  2.49 us (3%)
  between operations  1.16 us (1%)
    pallas_call x1, Pallas kernels, legendre(): pl.pallas_call(kernel, grid=(chunks,), in_specs=[whole] * 9, out_specs=(p...  18.7 us
    pallas_call x1, Pallas kernels, fourier_both_ways(): pl.pallas_call(kernel, grid=(slots,), in_specs=[pl.BlockSpec(memory_space...  9.07 us
    all_to_all x1, starting transfers between devices, body(): lax.all_to_all(outgoing, ('band', 'lev'), split_axis=0, concat_axis=0, ti...  7.37 us
    all_to_all x1, waiting for transfers between devices, body(): lax.all_to_all(returning, ('band', 'lev'), split_axis=0, concat_axis=0, t...  6.21 us
    pallas_call x1, Pallas kernels, adjoint(): pl.pallas_call(kernel, grid=(pairs // cluster,), in_specs=[pl.BlockSpec((...  5.66 us
    all_to_all x1, starting transfers between devices, body(): lax.all_to_all(returning, ('band', 'lev'), split_axis=0, concat_axis=0, t...  3.51 us
    all_to_all x1, waiting for transfers between devices, body(): lax.all_to_all(outgoing, ('band', 'lev'), split_axis=0, concat_axis=0, ti...  3.12 us
    unnamed x14, local copies, waits for them, and re-layouts  2.91 us
  transfers between devices with their start and end apart: 2, of which 2 were waited for; matrix products, arithmetic and copies ran while one was open for 6% of the time, Pallas kernels for 0%

profile of v5, /device:TPU:0, one launch (start us, length us, event | category | flops | bytes accessed | tf_op | source)
XLA Modules:
  0.0 78.4 jit_solution(15367614864145359231)
XLA Ops:
  0.7 0.8 broadcast_subtract_fusion
  1.6 0.3 select_reduce_fusion
  2.4 0.1 add.152
  2.6 0.1 mul.126
  2.9 0.1 mul.134
  3.0 0.7 sine_log_fusion
  3.8 0.6 pad.32.refs_3_
  4.4 0.6 pad.33.refs_4_
  5.1 0.6 pad.30.refs_0_
  5.8 0.8 copy.45.refs_6_.refs_0_
  6.7 0.6 pad.34.refs_5_
  7.5 0.6 pad.31.refs_2_
  8.1 0.6 fusion.18.refs_7_.refs_1_
  8.7 1.1 %and_convert_fusion.refs_1_ = bf16[256,1280]{1,0:T(8,128)(2,1)} fusion(s32[1280]{0:T(1024)S(1)} %add_select_fusion.1, s32[256]{0:T(256)S(1)} %and_select_fusion.2, pred[256]{0:T(512)(128)(4,1)S(1)} %iota_compare_fusion.6), kind=kLoop, calls=%fused_computation.15 | loop fusion | flops 983040 | bytes 661760 | tf_op jit(solution)/shard_map/convert_element_type | solution.py:190
  9.8 18.7 %legendre.1 = (bf16[10,1296,256]{2,1,0:T(8,128)(2,1)}, f32[10,8,256]{2,1,0:T(8,128)}) custom-call(s32[2,256]{1,0:T(2,128)} %pad.30.refs_0_, bf16[256,1280]{1,0:T(8,128)(2,1)} %and_convert_fusion.refs_1_, f32[24,128]{1,0:T(8,128)} %pad.31.refs_2_, f32[24,128]{1,0:T(8,128)} %pad.32.refs_3_, f32[24,128]{1,0:T(8,128)} %pad.33.refs_4_, s32[24,128]{1,0:T(8,128)} %pad.34.refs_5_, ...), custom_call_target="tpu_custom_call" | custom-call | tf_op jit(solution)/shard_map/legendre/pallas_call | solution.py:199
  28.5 0.9 %convert_element_type.83 = bf16[10,8,256]{2,1,0:T(8,128)(2,1)S(1)} convert(f32[10,8,256]{2,1,0:T(8,128)} %get-tuple-element.6) | non-fusion elementwise | flops 20480 | bytes 122880 | tf_op jit(solution)/shard_map/convert_element_type | solution.py:415
  29.5 0.3 reshape.257
  29.7 0.3 copy.46
  30.1 0.2 select_reduce_fusion.3
  30.3 0.3 convolution_convert_fusion
  30.6 0.8 %reshape.259 = bf16[16,8,320]{2,1,0:T(8,128)(2,1)} reshape(bf16[32,1280]{1,0:T(8,128)(2,1)S(1)} %convolution_convert_fusion) | data formatting | bytes 163840 | tf_op jit(solution)/shard_map/reshape | solution.py:421
  31.4 7.4 %all-to-all-start = ((bf16[16,8,320]{2,1,0:T(8,128)(2,1)}), bf16[16,8,320]{2,1,0:T(8,128)(2,1)S(1)}, u32[]{:S(2)}, u32[]{:S(2)}) async-start(bf16[16,8,320]{2,1,0:T(8,128)(2,1)} %reshape.259), calls=%async_computation | async-start | bytes 196608 | tf_op jit(solution)/shard_map/all_to_all | solution.py:422
  39.0 0.1 broadcast_in_dim.116
  39.1 0.2 reshape.262
  39.7 1.5 %fusion.13 = (f32[2,104,128]{2,1,0:T(8,128)S(1)}, f32[2,104,128]{2,1,0:T(8,128)S(1)}) fusion(f32[2]{0:T(128)S(1)} %convert_divide_fusion, s32[2]{0:T(128)S(1)} %get-tuple-element.20, s32[104,128]{1,0:T(8,128)S(1)} %pad_add_fusion), kind=kLoop, calls=%fused_computation.24 | loop fusion | flops 212992 | bytes 266256 | tf_op jit(solution)/shard_map/sin | solution.py:363
  41.3 0.3 copy.50
  41.7 0.3 copy.52
  42.0 0.1 copy.53
  42.1 0.2 copy.54
  42.2 0.1 copy.55
  42.3 0.2 copy.56
  42.5 0.1 tile.23
  42.7 3.1 %all-to-all-done = bf16[16,8,320]{2,1,0:T(8,128)(2,1)S(1)} async-done(((bf16[16,8,320]{2,1,0:T(8,128)(2,1)}), bf16[16,8,320]{2,1,0:T(8,128)(2,1)S(1)}, u32[]{:S(2)}, u32[]{:S(2)}) %all-to-all-start) | async-done | bytes 81952 | tf_op jit(solution)/shard_map/all_to_all | solution.py:422
  46.0 0.1 reshape.261
  46.1 0.8 %fusion.8 = bf16[32,1280]{1,0:T(8,128)(2,1)S(1)} fusion(bf16[32,1280]{1,0:T(8,128)(2,1)S(1)} %reshape.261, bf16[1280]{0:T(1024)(128)(2,1)S(1)} %fusion.27, s32[1280]{0:T(1024)S(1)} %subtract_select_fusion), kind=kOutput, calls=%fused_computation.10 | convolution fusion | flops 108175360 | bytes 171520 | tf_op jit(solution)/shard_map/dot_general | solution.py:431
  47.1 9.1 %fourier.1 = (f32[2,2,4,5376]{3,2,1,0:T(4,128)S(1)}, bf16[2,80,256]{2,1,0:T(8,128)(2,1)S(1)}) custom-call(s32[2]{0:T(128)S(1)} %get-tuple-element.21.refs_0_, bf16[2,80,256]{2,1,0:T(8,128)(2,1)S(1)} %reshape.264.refs_1_, f32[2,8,5376]{2,1,0:T(8,128)S(1)} %pad.35.refs_2_, f32[2,88,128]{2,1,0:T(8,128)S(1)} %slice.40.refs_3_, f32[2,88,128]{2,1,0:T(8,128)S(1)} %slice.41.refs_4_, ...), custom_call_target="tpu_custom_call" | custom-call | tf_op jit(solution)/shard_map/fourier/pallas_call | solution.py:378
  56.3 1.2 %fusion.9 = bf16[32,1280]{1,0:T(8,128)(2,1)S(1)} fusion(bf16[1280]{0:T(1024)(128)(2,1)S(1)} %fusion.27, s32[1280]{0:T(1024)S(1)} %subtract_select_fusion, bf16[4,8,10,128]{3,2,1,0:T(8,128)(2,1)S(1)} %bitcast.51), kind=kOutput, calls=%fused_computation.11 | convolution fusion | flops 108175360 | bytes 171520 | tf_op jit(solution)/shard_map/dot_general | solution.py:442
  57.4 0.2 reshape.271
  57.7 0.7 reshape.272
  58.4 3.5 %all-to-all-start.1 = ((bf16[16,8,320]{2,1,0:T(8,128)(2,1)}), bf16[16,8,320]{2,1,0:T(8,128)(2,1)S(1)}, u32[]{:S(2)}, u32[]{:S(2)}) async-start(bf16[16,8,320]{2,1,0:T(8,128)(2,1)} %reshape.272), calls=%async_computation.1 | async-start | bytes 196608 | tf_op jit(solution)/shard_map/all_to_all | solution.py:447
  61.9 0.8 slice.39
  62.7 6.2 %all-to-all-done.1 = bf16[16,8,320]{2,1,0:T(8,128)(2,1)S(1)} async-done(((bf16[16,8,320]{2,1,0:T(8,128)(2,1)}), bf16[16,8,320]{2,1,0:T(8,128)(2,1)S(1)}, u32[]{:S(2)}, u32[]{:S(2)}) %all-to-all-start.1) | async-done | bytes 81952 | tf_op jit(solution)/shard_map/all_to_all | solution.py:447
  68.9 0.1 reshape.273
  69.0 0.2 fusion.10
  69.2 0.2 copy.59
  69.5 0.3 reshape.274.refs_2_
  69.9 2.9 %copy-done = bf16[10,1296,256]{2,1,0:T(8,128)(2,1)S(1)} copy-done((bf16[10,1296,256]{2,1,0:T(8,128)(2,1)S(1)}, bf16[10,1296,256]{2,1,0:T(8,128)(2,1)}, u32[]{:S(2)}) %copy-start) | copy-done | bytes 6635544
  72.7 5.7 %adjoint.1 = bf16[2,2,160,1281]{3,2,1,0:T(8,128)(2,1)} custom-call(s32[160,1]{1,0:T(8,128)S(1)} %copy-done.1, f32[16,256]{1,0:T(8,128)S(1)} %copy-done.2, f32[10,8,256]{2,1,0:T(8,128)S(1)} %reshape.274.refs_2_, bf16[10,1296,256]{2,1,0:T(8,128)(2,1)S(1)} %copy-done), custom_call_target="tpu_custom_call" | custom-call | tf_op jit(solution)/shard_map/adjoint/pallas_call | solution.py:231
  (82 shorter events, 2.7 us)
Async XLA Ops:
  0.6 29.4 %copy-start.5 = (s32[16]{0:T(128)S(1)}, s32[16]{0:T(128)}, u32[]{:S(2)}) copy-start(s32[16]{0:T(128)} %param.9) | copy-start | bytes 196
  2.0 36.9 %copy-start.6 = (s32[16]{0:T(128)S(1)}, s32[16]{0:T(128)}, u32[]{:S(2)}) copy-start(s32[16]{0:T(128)} %param.7) | copy-start | bytes 196
  2.0 37.0 %copy-start.4 = (s32[640]{0:T(1024)S(1)}, s32[640]{0:T(1024)}, u32[]{:S(2)}) copy-start(s32[640]{0:T(1024)} %param.8) | copy-start | bytes 7684
  28.5 14.0 %copy-start.3 = (bf16[2,4,5136]{2,1,0:T(4,128)(2,1)S(1)}, bf16[2,4,5136]{2,1,0:T(4,128)(2,1)}, u32[]{:S(2)}) copy-start(bf16[2,4,5136]{2,1,0:T(4,128)(2,1)} %param.6) | copy-start | bytes 246532
  31.4 14.4 %all-to-all-start = ((bf16[16,8,320]{2,1,0:T(8,128)(2,1)}), bf16[16,8,320]{2,1,0:T(8,128)(2,1)S(1)}, u32[]{:S(2)}, u32[]{:S(2)}) async-start(bf16[16,8,320]{2,1,0:T(8,128)(2,1)} %reshape.259), calls=%async_computation | async-start | bytes 196608 | tf_op jit(solution)/shard_map/all_to_all | solution.py:422
  57.4 12.4 %copy-start.1 = (s32[160,1]{1,0:T(8,128)S(1)}, s32[160,1]{1,0:T(8,128)}, u32[]{:S(2)}) copy-start(s32[160,1]{1,0:T(8,128)} %copy.45.refs_6_.refs_0_) | copy-start | bytes 1924
  57.4 12.4 %copy-start.2 = (f32[16,256]{1,0:T(8,128)S(1)}, f32[16,256]{1,0:T(8,128)}, u32[]{:S(2)}) copy-start(f32[16,256]{1,0:T(8,128)} %fusion.18.refs_7_.refs_1_) | copy-start | bytes 49156
  58.4 10.5 %all-to-all-start.1 = ((bf16[16,8,320]{2,1,0:T(8,128)(2,1)}), bf16[16,8,320]{2,1,0:T(8,128)(2,1)S(1)}, u32[]{:S(2)}, u32[]{:S(2)}) async-start(bf16[16,8,320]{2,1,0:T(8,128)(2,1)} %reshape.272), calls=%async_computation.1 | async-start | bytes 196608 | tf_op jit(solution)/shard_map/all_to_all | solution.py:447
  69.8 2.9 %copy-start = (bf16[10,1296,256]{2,1,0:T(8,128)(2,1)S(1)}, bf16[10,1296,256]{2,1,0:T(8,128)(2,1)}, u32[]{:S(2)}) copy-start(bf16[10,1296,256]{2,1,0:T(8,128)(2,1)} %get-tuple-element.9.refs_3_) | copy-start | bytes 19906564
